TPU v7x, 32 devices: a whole 2x2x4 slice. The times are simulated.
32 devices in a mesh: dp: 16 (over z, y, x), group: 2 (over core).
Axes of the slice: x: 2, y: 2, z: 4, core: 2. Of those that a mesh axis runs over, the one named last changes fastest.
Arguments:
- tokens: bfloat16 [32, 1024, 768], P(('dp', 'group')), may hold values from -6 to 6
- segments: int32 [32, 1024], P(('dp', 'group')), may hold values from 0 to 7, never falling along the last dimension, each value on 1 to 256 neighbouring positions
- labels: int32 [32], P(('dp', 'group')), may hold values from 0 to 2, as said below
- cotangent: bfloat16 [32, 1024, 768], P(('dp', 'group')), may hold values from -6 to 6
- w_qkv: bfloat16 [768, 2304], replicated, may hold values from -0.21875 to 0.21875
- b_query: float32 [768], replicated, may hold values from -3 to 3
- b_value: float32 [768], replicated, may hold values from -3 to 3
- w_out: bfloat16 [768, 768], replicated, may hold values from -0.875 to 0.875
- b_out: float32 [768], replicated, may hold values from -2 to 2
- gamma_one: float32 [768], replicated, may hold values from 0.5 to 1.5
- beta_one: float32 [768], replicated, may hold values from -2 to 2
- gamma_two: float32 [768], replicated, may hold values from 0.5 to 1.5
- beta_two: float32 [768], replicated, may hold values from -2 to 2
- w_up: bfloat16 [768, 3072], replicated, may hold values from -0.21875 to 0.21875
- b_up: float32 [3072], replicated, may hold values from -3 to 3
- w_down: bfloat16 [3072, 768], replicated, may hold values from -0.109375 to 0.109375
- b_down: float32 [768], replicated, may hold values from -2 to 2
Outputs:
- mixed: bfloat16 [32, 1024, 768], P(('dp', 'group'))
- grad_tokens: bfloat16 [32, 1024, 768], P(('dp', 'group'))
- grad_w_qkv: float32 [768, 2304], P('dp')
- grad_b_query: float32 [768], P('dp')
- grad_b_value: float32 [768], P('dp')
- grad_w_out: float32 [768, 768], P('dp')
- grad_b_out: float32 [768], P('dp')
- grad_gamma_one: float32 [768], P('dp')
- grad_beta_one: float32 [768], P('dp')
- grad_gamma_two: float32 [768], P('dp')
- grad_beta_two: float32 [768], P('dp')
- grad_w_up: float32 [768, 3072], P('dp')
- grad_b_up: float32 [3072], P('dp')
- grad_w_down: float32 [3072, 768], P('dp')
- grad_b_down: float32 [768], P('dp')
- counts: int32 [3], replicated
Inputs may be any that keep to these rules, and one draw needn't show every extreme that they name: Taken in window order, the labels form 3 runs, one for each task, in an order that varies; each run covers whole consecutive indices of dp (all windows of a device and of both cores of a chip share a label) and at least max(1, 2) of them, so every task has windows.
All inputs are finite; a program needn't handle non-finite values.
Results may differ from a plain program's by a relative error of at most 0.015.
Values sent between devices are 32-bit elements; how exact they have to be, the bound alone decides.
No kernel may reach another device: no remote copies, remote signals or barrier semaphores. Data moves between devices by JAX's collectives and lax.ppermute only.
A program may use at most 256 MiB of HBM per device.

v0:
```python
import functools
import math

import jax
import jax.numpy as jnp
from jax import lax
from jax.experimental import pallas as pl
from jax.experimental.pallas import tpu as pltpu
from jax.sharding import PartitionSpec as P

F32 = jnp.float32
BF = jnp.bfloat16
D = 768
HEADS = 12
HEAD = 64
PAIR = 2 * HEAD
LANES = 128
FF = 3072
NTASK = 3
VECTORS = 16
QB = 256
EPISODE = 256
QUERIES = 128
STAGGER = 2
HALF = D // 2
AXES = ("dp", "group")
NN = (((1,), (0,)), ((), ()))
NT = (((1,), (1,)), ((), ()))
TN = (((0,), (0,)), ((), ()))
PLAN = {'D': [(3, ((1, 2, 3, 0), (0, 2, 3, 1))), (1, ((2, 3, 1, 0), (2, 3, 0, 1)))], 'U': [(3, ((0, 1, 2, 3), (1, 0, 2, 3))), (1, ((2, 0, 1, 3), (2, 1, 0, 3)))], 'F': [(3, ((1, 2, 0, 3), (0, 2, 1, 3))), (6, ((1, 0, 2, 3), (0, 1, 2, 3)))], 'L': [(3, ((0, 1, 2, 3), (1, 0, 2, 3)))]}
SCHEDULE = ['hidden', ('D0', 'D1'), 'middle', ('U0', 'U1', 'D1'), 'attend first', ('D0',), 'first heads', ('D1',), ('U0',), 'attend last', ('D1', 'U1', 'F0', 'F1'), 'last heads', ('U0',), ('D0',), 'input', ('U1', 'F0', 'L0', 'D1'), ('V',), ('U0', 'U1'), ('F1',), 'mix', ('D0', 'U1', 'F0', 'V'), ('U0', 'F1'), ('D0', 'F0', 'V'), ('L0',), ('L0', 'V', 'F0', 'F1'), ('V', 'L0'), ('F1', 'L0')]
SMALL_FLOPS = 1000000000
SMALL_LIMIT = 20 * 2**20
BIG = 1 << 40
COST = {'first_heads_grad': 0, 'last_heads_grad': 0, 'attend_back_first': 20, 'attend_back_last': 20, 'norm_one_back': 3, 'mix': 20, 'norm_two_back': 3}
FREE = {"hidden_grad": [6], "norm_two_back": [0, 3], "first_heads_grad": [1, 2], "last_heads_grad": [1, 2], "norm_one_back": [3, 4, 5], "mix": [2]}
OUT = {"up_and_down_grad": [2], "hidden_grad": [0, 1], "attend_back_first": [0], "attend_back_last": [0]}
VMEM_LIMIT = 34 * 2**20
SCALE = 1
FLOPS = 4e9


def dot(a, b, dims=NN):
    return lax.dot_general(a, b, dims, preferred_element_type=F32)


def in_hbm(x):
    return pltpu.with_memory_space_constraint(x, pltpu.HBM)


def call(kernel, name, grid, in_specs, out_specs, out_shape, scratch=(), prefetch=0, us=3, after=0, free=(), limit=None):
    in_specs = list(in_specs) + [pl.BlockSpec(memory_space=pl.ANY)] * after
    body = kernel
    if after:
        start = prefetch + len(in_specs) - after

        def body(*refs):
            kernel(*refs[:start], *refs[start + after :])

    single = not isinstance(out_shape, list)
    made = [(s if n in OUT.get(name, ()) else pltpu.HBM(s.shape, s.dtype)) if isinstance(s, jax.ShapeDtypeStruct) else s for n, s in enumerate([out_shape] if single else out_shape)]
    run = pl.pallas_call(
        body,
        grid_spec=pltpu.PrefetchScalarGridSpec(
            num_scalar_prefetch=prefetch,
            grid=grid,
            in_specs=in_specs,
            out_specs=[out_specs] if single else out_specs,
            scratch_shapes=list(scratch),
        ),
        out_shape=made,
        compiler_params=pltpu.CompilerParams(vmem_limit_bytes=limit or VMEM_LIMIT),
        cost_estimate=pl.CostEstimate(flops=int(COST.get(name, us) * FLOPS), bytes_accessed=int(us * SCALE), transcendentals=0),
        name=name,
    )

    def apply(*args):
        last = len(args) - after
        table = FREE.get(name, free)
        args = [x if n < prefetch or n >= last or n in table else in_hbm(x) for n, x in enumerate(args)]
        out = run(*args)
        return out[0] if single else out

    return apply


def shape(dims, dtype):
    return jax.ShapeDtypeStruct(dims, dtype)


def whole(*dims):
    return pl.BlockSpec(dims, lambda *_: (0,) * len(dims))


SMEM = pl.BlockSpec(memory_space=pltpu.SMEM)


def unit(x):
    centered = x - jnp.mean(x, axis=-1, keepdims=True)
    inv = lax.rsqrt(jnp.mean(centered * centered, axis=-1, keepdims=True) + 1e-05)
    return centered * inv, inv


def norm_back(e, u, inv, gain):
    scaled = e * gain
    return inv * (
        scaled
        - jnp.mean(scaled, axis=-1, keepdims=True)
        - u * jnp.mean(scaled * u, axis=-1, keepdims=True)
    )


def rows_of(ref):
    return range(0, ref.shape[0], QB)


def column_sum(x):
    return jnp.sum(x, axis=0, keepdims=True)


def bands(t):
    return [(q, max(0, q - EPISODE), min(q + QUERIES, EPISODE + QUERIES)) for q in range(0, t, QUERIES)]


def head_pair(x):
    lane = lax.broadcasted_iota(jnp.int32, (1, PAIR), 1)
    zero = jnp.zeros_like(x)
    return jnp.concatenate([jnp.where(lane < HEAD, x, zero), jnp.where(lane < HEAD, zero, x)], axis=0)


def heads_side_by_side(x):
    return jnp.concatenate([x[:HEAD, :QUERIES], x[HEAD:, QUERIES:]], axis=0).T


def staggered(units, stages):
    waiting = [{} for _ in stages]
    lags = [0, STAGGER, STAGGER + 1]
    for n in range(len(units) + lags[-1]):
        for k, stage in enumerate(stages):
            m = n - lags[k]
            if 0 <= m < len(units):
                given = () if k == 0 else (waiting[k - 1].pop(m),)
                waiting[k][m] = stage(*units[m], *given)


def forward_kernel(x_ref, seg_ref, g1_ref, s1_ref, wq_ref, wk_ref, wv_ref, bq_ref, bv_ref, wo_ref, bo_ref, g2_ref, s2_ref, proj_ref, in_one_ref, att_ref, p_ref, mid_ref, in_two_ref, bias_ref, turned_ref, acc_ref):
    g = pl.program_id(0)
    t = x_ref.shape[0]
    blocks = bands(t)

    @pl.when(g == 0)
    def _():
        for r in rows_of(x_ref):
            u, _ = unit(x_ref[r : r + QB].astype(F32))
            in_one_ref[r : r + QB] = (u * g1_ref[...] + s1_ref[...]).astype(BF)
            acc_ref[r : r + QB] = x_ref[r : r + QB].astype(F32) + bo_ref[...]
        hot = (seg_ref[...] == lax.broadcasted_iota(jnp.int32, (8, t), 0)).astype(BF)
        for i, (q0, k0, n) in enumerate(blocks):
            same = dot(hot[:, k0 : k0 + n], hot[:, q0 : q0 + QUERIES], TN)
            col = k0 + lax.broadcasted_iota(jnp.int32, (n, QUERIES), 0)
            row = q0 + lax.broadcasted_iota(jnp.int32, (n, QUERIES), 1)
            bias_ref[i, :n] = jnp.where((same > 0.5) & (col <= row), 0.0, -1e30).astype(F32)

    width = wq_ref.shape[1]
    here = pl.ds(pl.multiple_of(g * width, width), width)
    for r in range(0, t, 2 * QB):
        rows = in_one_ref[r : r + 2 * QB]
        proj_ref[0, r : r + 2 * QB] = ((dot(rows, wq_ref[...]) + bq_ref[here]) * HEAD**-0.5).astype(BF)
        proj_ref[1, r : r + 2 * QB] = dot(rows, wk_ref[...]).astype(BF)
        proj_ref[2, r : r + 2 * QB] = (dot(rows, wv_ref[...]) + bv_ref[here]).astype(BF)
    pairs = width // PAIR
    for w in range(pairs):
        turned_ref[w] = proj_ref[2, :, w * PAIR : (w + 1) * PAIR].T

    def scores(w, i):
        q0, k0, n = blocks[i]
        cols = slice(w * PAIR, (w + 1) * PAIR)
        return dot(proj_ref[1, k0 : k0 + n, cols], head_pair(proj_ref[0, q0 : q0 + QUERIES, cols]), NT)

    def softmax(w, i, values):
        n = blocks[i][2]
        parts = []
        for a in range(2):
            part = values[:, a * QUERIES : (a + 1) * QUERIES] + bias_ref[i, :n]
            e = jnp.exp(part - jnp.max(part, axis=0, keepdims=True))
            probs = (e * (1.0 / jnp.sum(e, axis=0, keepdims=True))).astype(BF)
            p_ref[w, i, :n, a * QUERIES : (a + 1) * QUERIES] = probs
            parts.append(probs)
        return jnp.concatenate(parts, axis=1)

    def attend(w, i, probs):
        q0, k0, n = blocks[i]
        out = dot(turned_ref[w, :, k0 : k0 + n], probs)
        att_ref[q0 : q0 + QUERIES, w * PAIR : (w + 1) * PAIR] = heads_side_by_side(out).astype(BF)

    units = [(w, i) for w in range(pairs) for i in range(len(blocks))]
    staggered(units, (scores, softmax, attend))

    acc_ref[...] += dot(att_ref[...], wo_ref[...])

    @pl.when(g == pl.num_programs(0) - 1)
    def _():
        for r in rows_of(x_ref):
            mid = acc_ref[r : r + QB]
            mid_ref[r : r + QB] = mid
            u, _ = unit(mid)
            in_two_ref[r : r + QB] = (u * g2_ref[...] + s2_ref[...]).astype(BF)


def forward(x, seg, gain_one, shift_one, w_qkv, b_query, b_value, w_out, b_out, gain_two, shift_two):
    t = x.shape[0]
    width = 2 * PAIR
    steps = D // width
    count = t // QUERIES
    keys = EPISODE + QUERIES

    def weights(part):
        return pl.BlockSpec((D, width), lambda g: (0, part * steps + g))

    return call(
        forward_kernel,
        "forward",
        (steps,),
        [whole(t, D), whole(1, t), whole(D), whole(D), weights(0), weights(1), weights(2), whole(D), whole(D)]
        + [pl.BlockSpec((width, D), lambda g: (g, 0)), whole(D), whole(D), whole(D)],
        [
            pl.BlockSpec((3, t, width), lambda g: (0, 0, g)),
            whole(t, D),
            pl.BlockSpec((t, width), lambda g: (0, g)),
            pl.BlockSpec((2, count, keys, 2 * QUERIES), lambda g: (g, 0, 0, 0)),
            whole(t, D),
            whole(t, D),
        ],
        [
            shape((3, t, D), BF),
            shape((t, D), BF),
            shape((t, D), BF),
            shape((HEADS // 2, count, keys, 2 * QUERIES), BF),
            shape((t, D), F32),
            shape((t, D), BF),
        ],
        [
            pltpu.VMEM((count, keys, QUERIES), F32),
            pltpu.VMEM((2, PAIR, t), BF),
            pltpu.VMEM((t, D), F32),
        ],
        us=24,
        limit=60 * 2**20,
    )(x, seg, gain_one, shift_one, w_qkv, w_qkv, w_qkv, b_query, b_value, w_out, b_out, gain_two, shift_two)


def gelu_both(v):
    cdf = 0.5 * (1.0 + lax.erf(v * (2.0**-0.5)))
    pdf = jnp.exp(-0.5 * v * v) * (1.0 / math.sqrt(2 * math.pi))
    return v * cdf, cdf + v * pdf


def own_first(core, x):
    half = x.shape[1] // 2
    return jnp.where(core == 0, x, jnp.concatenate([x[:, half:], x[:, :half]], axis=1))


def task_weight(counts_ref, label_ref, width):
    total = (counts_ref[0] + counts_ref[1] + counts_ref[2]).astype(F32)
    here = (NTASK * counts_ref[label_ref[0]]).astype(F32)
    return jnp.full((1, width), total, F32) / jnp.full((1, width), here, F32)


def up_kernel(pos_ref, in_ref, cot_ref, w_ref, b_ref, act_ref, slope_ref, own_ref, other_ref, turned):
    @pl.when(pl.program_id(0) == 0)
    def _():
        turned[...] = own_first(pos_ref[1], cot_ref[...])

    bias = b_ref[pl.ds(pl.multiple_of(pl.program_id(0) * D, D), D)]
    rows = QB // 2
    starts = list(range(0, in_ref.shape[0], rows))
    pre = None
    for r in starts + [None]:
        ready, pre = pre, None if r is None else dot(in_ref[r : r + rows], w_ref[...]) + bias
        if ready is not None:
            act, slope = gelu_both(ready)
            act_ref[last : last + rows] = act.astype(BF)
            slope_ref[last : last + rows] = slope.astype(BF)
        last = r
    grad = dot(act_ref[...], turned[...], TN)
    own_ref[...] = grad[:, :HALF]
    other_ref[...] = grad[:, HALF:]


def up(pos, in_two, cot, w_up, b_up, after=()):
    t = in_two.shape[0]
    cols = pl.BlockSpec((t, D), lambda j, *_: (0, j))
    half = pl.BlockSpec((D, HALF), lambda j, *_: (j, 0))
    return call(
        up_kernel,
        "up_and_down_grad",
        (FF // D,),
        [
            whole(t, D),
            whole(t, D),
            pl.BlockSpec((D, D), lambda j, *_: (0, j)),
            whole(FF),
        ],
        [cols, cols, half, half],
        [shape((t, FF), BF)] * 2 + [shape((FF, HALF), F32)] * 2,
        [pltpu.VMEM((t, D), BF)],
        prefetch=1,
        us=16,
        after=len(after),
    )(pos, in_two, cot, w_up, b_up, *after)


def hidden_kernel(pos_ref, counts_ref, label_ref, cot_ref, in_ref, slope_ref, w_ref, gp_ref, go_ref, own_ref, other_ref, sum_ref, down_ref):
    @pl.when(pl.program_id(0) == 0)
    def _():
        go = (cot_ref[...].astype(F32) * task_weight(counts_ref, label_ref, D)).astype(BF)
        go_ref[...] = go
        down_ref[...] = column_sum(go.astype(F32))

    grad = None
    for r in list(rows_of(go_ref)) + [None]:
        ready, grad = grad, None if r is None else dot(go_ref[r : r + QB], w_ref[...], NT)
        if ready is not None:
            gp_ref[last : last + QB] = (ready * slope_ref[last : last + QB].astype(F32)).astype(BF)
        last = r
    sum_ref[0] = column_sum(gp_ref[...].astype(F32))
    grad = dot(in_ref[...], own_first(pos_ref[1], gp_ref[...]), TN)
    own_ref[0] = grad[:, :HALF]
    other_ref[0] = grad[:, HALF:]


def block_half():
    return pl.BlockSpec((1, D, HALF), lambda j, *_: (j, 0, 0))


def hidden(pos, counts, labels, cot, in_two, slope, w_down):
    t = in_two.shape[0]
    cols = pl.BlockSpec((t, D), lambda j, *_: (0, j))
    return call(
        hidden_kernel,
        "hidden_grad",
        (FF // D,),
        [whole(t, D), whole(t, D), cols, pl.BlockSpec((D, D), lambda j, *_: (j, 0))],
        [
            cols,
            whole(t, D),
            block_half(),
            block_half(),
            pl.BlockSpec((1, 1, D), lambda j, *_: (j, 0, 0)),
            whole(1, D),
        ],
        [shape((t, FF), BF), shape((t, D), BF)]
        + [shape((FF // D, D, HALF), F32)] * 2
        + [shape((FF // D, 1, D), F32), shape((1, D), F32)],
        prefetch=3,
        us=14,
    )(pos, counts, labels, cot, in_two, slope, w_down)


def add_sums(ref, first, sums):
    for n, value in enumerate(sums):

        @pl.when(first)
        def _():
            ref[n : n + 1] = value

        @pl.when(jnp.logical_not(first))
        def _():
            ref[n : n + 1] += value


def middle_kernel(go_ref, mid_ref, g_ref, gp_ref, wu_ref, wo_ref, gm_ref, gb_ref, ga_ref, sums_ref):
    starts = rows_of(gm_ref)
    following = dot(gp_ref[:QB], wu_ref[...], NT)
    sums = [0.0, 0.0, 0.0]
    for r in starts:
        e = following
        if r + QB < gm_ref.shape[0]:
            following = dot(gp_ref[r + QB : r + 2 * QB], wu_ref[...], NT)
        u, inv = unit(mid_ref[r : r + QB])
        gm = go_ref[r : r + QB].astype(F32) + norm_back(e, u, inv, g_ref[...])
        gm_ref[r : r + QB] = gm
        gb = gm.astype(BF)
        gb_ref[r : r + QB] = gb
        ga_ref[r : r + QB] = dot(gb, wo_ref[...], NT).astype(BF)
        parts = (column_sum(e * u), column_sum(e), column_sum(gb.astype(F32)))
        sums = [total + part for total, part in zip(sums, parts)]
    add_sums(sums_ref, pl.program_id(0) == 0, sums)


def middle_back(go, mid, gain, gp, w_up, w_out, after=()):
    t = go.shape[0]
    rows = 2 * QB
    row = pl.BlockSpec((rows, D), lambda i: (i, 0))
    return call(
        middle_kernel,
        "norm_two_back",
        (t // rows,),
        [row, row, whole(D), pl.BlockSpec((rows, FF), lambda i: (i, 0)), whole(D, FF), whole(D, D)],
        [row, row, row, whole(3, D)],
        [shape((t, D), F32), shape((t, D), BF), shape((t, D), BF), shape((3, D), F32)],
        us=16,
        after=len(after),
    )(go, mid, gain, gp, w_up, w_out, *after)


def attend_back_kernel(q_ref, k_ref, v_ref, ga_ref, p_ref, d_ref, dk_ref, dv_ref, turned_ref):
    t = q_ref.shape[1]
    blocks = bands(t)

    @pl.loop(0, q_ref.shape[2] // PAIR)
    def _(w):
        cols = pl.ds(pl.multiple_of(w * PAIR, PAIR), PAIR)
        turned_ref[...] = k_ref[0, :, cols].T

        def grad_probs(i):
            q0, k0, n = blocks[i]
            return dot(v_ref[0, k0 : k0 + n, cols], head_pair(ga_ref[q0 : q0 + QUERIES, cols]), NT)

        def grad_scores(i, values):
            probs = p_ref[w, i, : blocks[i][2]].astype(F32)
            prod = probs * values
            return (prod - probs * jnp.sum(prod, axis=0, keepdims=True)).astype(BF)

        def rest(i, ds):
            q0, k0, n = blocks[i]
            dq = heads_side_by_side(dot(turned_ref[:, k0 : k0 + n], ds))
            d_ref[0, q0 : q0 + QUERIES, cols] = dq.astype(BF) * jnp.asarray(HEAD**-0.5, BF)
            known = n - QUERIES if i else 0
            done = blocks[i + 1][1] if i + 1 < len(blocks) else t
            dk = dot(ds, head_pair(q_ref[0, q0 : q0 + QUERIES, cols]))
            dv = dot(p_ref[w, i, :n], head_pair(ga_ref[q0 : q0 + QUERIES, cols]))
            for part, ref, value in ((1, dk_ref, dk), (2, dv_ref, dv)):
                if known:
                    ref[k0 : k0 + known] += value[:known]
                ref[k0 + known : k0 + n] = value[known:]
                if done > k0:
                    d_ref[part, k0:done, cols] = ref[k0:done].astype(BF)

        staggered([(i,) for i in range(len(blocks))], (grad_probs, grad_scores, rest))


def attend_back(proj, ga, probs, first, pairs, after=()):
    t = proj.shape[1]
    width = 2 * PAIR
    start = first // 2

    def block(part):
        return pl.BlockSpec((1, t, width), lambda h: (part, 0, start + h))

    return call(
        attend_back_kernel,
        "attend_back_last" if first else "attend_back_first",
        (pairs // 2,),
        [
            block(0),
            block(1),
            block(2),
            pl.BlockSpec((t, width), lambda h: (0, start + h)),
            pl.BlockSpec((2,) + probs.shape[1:], lambda h: (start + h, 0, 0, 0)),
        ],
        pl.BlockSpec((3, t, width), lambda h: (0, 0, h)),
        shape((3, t, pairs * PAIR), BF),
        [pltpu.VMEM((t, PAIR), F32)] * 2 + [pltpu.VMEM((PAIR, t), BF)],
        us=3 * pairs,
        after=len(after),
    )(proj, proj, proj, ga, probs, *after)


def first_heads_kernel(pos_ref, in_ref, d_ref, att_ref, gb_ref, own_ref, other_ref):
    core = pos_ref[1]
    grad = dot(in_ref[...], own_first(core, d_ref[0]), TN)
    grad_out = dot(att_ref[...], own_first(core, gb_ref[...]), TN)
    columns = [grad[:, n * LANES : (n + 1) * LANES] for n in range(4)]
    columns += [grad_out[:, n * LANES : (n + 1) * LANES] for n in range(2)]
    for n, (own, other) in enumerate([(0, 2), (1, 3), (4, 5)]):
        own_ref[n] = columns[own]
        other_ref[n] = columns[other]


def first_heads(pos, in_one, d, att, gb, after=()):
    t = in_one.shape[0]
    block = pl.BlockSpec((3, D, LANES), lambda j, *_: (j, 0, 0))
    return call(
        first_heads_kernel,
        "first_heads_grad",
        (3,),
        [
            whole(t, D),
            pl.BlockSpec((1, t, 4 * LANES), lambda j, *_: (j, 0, 0)),
            whole(t, D),
            pl.BlockSpec((t, 2 * LANES), lambda j, *_: (0, j)),
        ],
        [block, block],
        [shape((9, D, LANES), F32)] * 2,
        prefetch=1,
        us=10,
        after=len(after),
    )(pos, in_one, d, att, gb, *after)


def last_heads_kernel(pos_ref, in_ref, d_ref, own_ref, other_ref):
    turned = jnp.concatenate([own_first(pos_ref[1], d_ref[b]) for b in range(3)], axis=1)
    grad = dot(in_ref[...], turned, TN)
    for b in range(3):
        own_ref[b] = grad[:, 2 * b * LANES : (2 * b + 1) * LANES]
        other_ref[b] = grad[:, (2 * b + 1) * LANES : (2 * b + 2) * LANES]


def last_heads(pos, in_one, d, after=()):
    t = in_one.shape[0]
    return call(
        last_heads_kernel,
        "last_heads_grad",
        (1,),
        [whole(t, D), whole(3, t, 2 * LANES)],
        [whole(3, D, LANES)] * 2,
        [shape((3, D, LANES), F32)] * 2,
        prefetch=1,
        us=5,
        after=len(after),
    )(pos, in_one, d, *after)


def input_kernel(x_ref, gm_ref, g_ref, first_ref, last_ref, w_ref, mid_sums, down_sum, up_sums, gt_ref, sums_ref):
    e = 0.0
    split = first_ref.shape[2]
    for b in range(3):
        e = e + dot(first_ref[b], w_ref[:, b * D : b * D + split], NT)
        e = e + dot(last_ref[b], w_ref[:, b * D + split : (b + 1) * D], NT)
    u, inv = unit(x_ref[...].astype(F32))
    gt_ref[...] = (gm_ref[...] + norm_back(e, u, inv, g_ref[...])).astype(BF)
    start = pl.program_id(0) == 0
    sums = []
    for b in (0, 2):
        pair = [column_sum(ref[b].astype(F32)) for ref in (first_ref, last_ref)]
        sums.append(jnp.concatenate(pair, axis=1))
    add_sums(sums_ref, start, sums + [column_sum(e * u), column_sum(e)])

    @pl.when(start)
    def _():
        sums_ref[4:7] = mid_sums[...]
        sums_ref[7:8] = down_sum[...]
        for b in range(FF // D):
            sums_ref[8 + b : 9 + b] = up_sums[b]
        sums_ref[8 + FF // D :] = jnp.zeros((VECTORS - 8 - FF // D, D), F32)


def input_back(x, gm, gain, first, last, w_qkv, mid_sums, down_sum, up_sums, after=()):
    t = x.shape[0]
    row = pl.BlockSpec((QB, D), lambda i: (i, 0))
    part = lambda d: pl.BlockSpec((3, QB, d.shape[2]), lambda i: (0, i, 0))
    return call(
        input_kernel,
        "norm_one_back",
        (t // QB,),
        [
            row,
            row,
            whole(D),
            part(first),
            part(last),
            whole(D, 3 * D),
            whole(3, D),
            whole(1, D),
            whole(FF // D, 1, D),
        ],
        [row, whole(VECTORS, D)],
        [shape((t, D), BF), shape((VECTORS, D), F32)],
        us=10,
        after=len(after),
    )(x, gm, gain, first, last, w_qkv, mid_sums, down_sum, up_sums, *after)


def mix_kernel(mid_ref, act_ref, w_ref, b_ref, out_ref):
    out_ref[...] = (mid_ref[...] + dot(act_ref[...], w_ref[...]) + b_ref[...]).astype(BF)


def mix(mid, act, w_down, b_down, after=()):
    t = mid.shape[0]
    row = pl.BlockSpec((QB, D), lambda i: (i, 0))
    return call(
        mix_kernel,
        "mix",
        (t // QB,),
        [row, pl.BlockSpec((QB, FF), lambda i: (i, 0)), whole(FF, D), whole(D)],
        row,
        shape((t, D), BF),
        us=10,
        after=len(after),
    )(mid, act, w_down, b_down, *after)


def swap_with(x, n_dp, masks):
    pairs = []
    for dp in range(n_dp):
        for core in range(2):
            mask = masks[core]
            target = (dp ^ mask) * 2 + core if mask else dp * 2 + 1 - core
            pairs.append((dp * 2 + core, target))
    return lax.ppermute(x, AXES, pairs)


def in_vmem(x):
    return pltpu.with_memory_space_constraint(x, pltpu.VMEM)


def small_call(kernel, name, scalars, arrays, outs, after=()):
    n = len(scalars) + len(arrays)

    def body(*refs):
        kernel(*refs[:n], *refs[n + len(after) :])

    vmem = pl.BlockSpec(memory_space=pltpu.VMEM)
    return pl.pallas_call(
        body,
        in_specs=[SMEM] * len(scalars) + [vmem] * len(arrays) + [pl.BlockSpec(memory_space=pl.ANY)] * len(after),
        out_specs=[vmem] * len(outs),
        out_shape=outs,
        compiler_params=pltpu.CompilerParams(vmem_limit_bytes=SMALL_LIMIT),
        cost_estimate=pl.CostEstimate(flops=SMALL_FLOPS, bytes_accessed=1, transcendentals=0),
        name=name,
    )(*scalars, *[in_vmem(x) if x.size < BIG else x for x in arrays], *[in_hbm(a) if a.dtype == BF or a.ndim < 4 else a for a in after])


class Stream:
    def __init__(self, n_dp, orders, pairs, names, step=0, weighted=False):
        self.n_dp, self.orders, self.pairs, self.step = n_dp, orders, pairs, step
        self.names = names
        self.weighted = weighted
        self.steps = len(orders[0])

    def __add__(self, other):
        assert self.step == other.step and self.orders == other.orders
        return Stream(
            self.n_dp, self.orders, self.pairs + other.pairs, self.names + other.names, self.step, self.weighted
        )

    def key(self):
        return (self.step, self.orders, self.weighted, self.pairs[0][0].shape[2:])

    @property
    def last(self):
        return self.step == self.steps

    @property
    def dims(self):
        count = 1 if self.last else self.n_dp >> (self.step + 1)
        return (count, sum(p[4] for p in self.pairs)) + self.pairs[0][0].shape[2:]

    def bit(self, core, j):
        a, b = self.orders[0][j], self.orders[1][j]
        return a if a == b else jnp.where(core == 0, a, b)

    def read(self, ref, pair, i, dp, core, mine):
        kind, first, size = pair[2:]
        if self.last:
            return ref[0, pl.ds(first, size)]
        bit = (dp >> self.bit(core, self.step)) & 1
        chosen = bit if mine else 1 - bit
        if kind == "kept":
            return ref[2 * i + chosen, pl.ds(first, size)]
        at = chosen << self.bit(core, 0)
        for j in range(1, self.steps):
            at = at + (((i >> (j - 1)) & 1) << self.bit(core, j))
        if kind == "rows":
            return ref[at, pl.ds(first, size)]
        return ref[pl.ds(first, size), at]


class Vectors:
    def __init__(self, total, n_dp):
        self.n_dp, self.total = n_dp, total
        self.masks = [0] + [1 << b for b in range(n_dp.bit_length() - 1)]
        self.swap()

    def swap(self):
        mask = self.masks.pop(0)
        self.received = swap_with(self.total, self.n_dp, (mask, mask))


def tick(pos, task, name, streams, after=(), vectors=None):
    arrays, jobs, outs = [], [], []

    def operand(array):
        for n, known in enumerate(arrays):
            if known is array:
                return n
        arrays.append(array)
        return len(arrays) - 1

    for stream in streams:
        pairs = [(operand(p[0]), operand(p[1])) for p in stream.pairs]
        jobs.append((stream, pairs, len(outs)))
        outs += [pltpu.VMEM(stream.dims, F32)] * (1 if stream.last else 2)
    if vectors is not None:
        pair = (operand(vectors.total), operand(vectors.received))
        outs.append(pltpu.VMEM((VECTORS, D), F32))

    scalars = [pos] + (list(task) if any(stream.weighted for stream in streams) else [])

    def kernel(pos_ref, *refs):
        task_refs, refs = refs[: len(scalars) - 1], refs[len(scalars) - 1 :]
        ins, out_refs = refs[: len(arrays)], refs[len(arrays) :]
        dp, core = pos_ref[0], pos_ref[1]

        def add(stream, pairs, n, mine, i):
            offset = 0
            for pair, (held, received) in zip(stream.pairs, pairs):
                a = stream.read(ins[held], pair, i, dp, core, mine)
                b = stream.read(ins[received], pair, i, dp, core, mine)
                total = a + b
                if stream.weighted:
                    total = total * task_weight(*task_refs, total.shape[-1])
                out_refs[n + mine][i, pl.ds(offset, pair[4])] = total
                offset += pair[4]

        for stream, pairs, n in jobs:
            for mine in (0,) if stream.last else (0, 1):
                act = functools.partial(add, stream, pairs, n, mine)
                if stream.dims[0] <= 8:
                    for i in range(stream.dims[0]):
                        act(i)
                else:
                    pl.loop(0, stream.dims[0])(act)
        if vectors is not None:
            out_refs[-1][...] = ins[pair[0]][...] + ins[pair[1]][...]

    return small_call(kernel, name, scalars, arrays, outs, after)


class Transfers:
    def __init__(self, pos, task, n_dp):
        self.pos, self.task, self.n_dp, self.ticks = pos, task, n_dp, 0
        self.streams, self.vectors, self.mine = [], None, []

    def other_core(self, value):
        return swap_with(value, self.n_dp, (0, 0))

    def order(self, pattern):
        return tuple(b for p in pattern for b in ([p] if p < 3 else range(3, self.n_dp.bit_length() - 1)))

    def begin(self, kind, own, other, names, plan, weighted):
        rows = D // self.n_dp
        blocks, width = len(names), own.shape[-1]
        dims = (self.n_dp, blocks, rows, width) if kind == "rows" else (blocks, self.n_dp, rows, width)
        own, received = own.reshape(dims), self.other_core(other.reshape(dims))
        first = 0
        for count, patterns in plan:
            orders = tuple(self.order(p) for p in patterns)
            pair = (own, received, kind, first, count)
            self.streams.append(Stream(self.n_dp, orders, [pair], names[first : first + count], weighted=weighted))
            first += count

    def named(self, name):
        return next((s for s in self.streams if name in s.names), None)

    def tick(self, wanted, after):
        vectors = None
        streams = []
        for name in wanted:
            if name == "vectors":
                vectors = self.vectors
                continue
            stream = self.named(name)
            if stream is not None and stream not in streams:
                streams.append(stream)
        merged = {}
        for stream in streams:
            self.streams.remove(stream)
            key = stream.key()
            merged[key] = merged[key] + stream if key in merged else stream
        streams = list(merged.values())
        self.ticks += 1
        sent = tick(self.pos, self.task, "tick_%d" % self.ticks, streams, after, vectors)
        n = 0
        for stream in streams:
            if stream.last:
                self.mine.append((sent[n], self.other_core(sent[n]), stream.names))
                n += 1
                continue
            masks = tuple(1 << order[stream.step] for order in stream.orders)
            received = swap_with(sent[n], self.n_dp, masks)
            pair = (sent[n + 1], received, "kept", 0, stream.dims[1])
            self.streams.append(Stream(self.n_dp, stream.orders, [pair], stream.names, stream.step + 1))
            n += 2
        if vectors is not None:
            vectors.total = sent[-1]
            if vectors.masks:
                vectors.swap()
            else:
                vectors.received = None
        return [sent[0]]

    def finish(self, after):
        while self.streams or self.vectors.received is not None:
            wanted = [s.names[0] for s in self.streams]
            after = self.tick(wanted + ["vectors"] * (self.vectors.received is not None), after)
        return after


def place_kernel(pos_ref, *refs, places, blocks, halves):
    core = pos_ref[1]
    for source, b, n, row, cols in places:
        mine, theirs = refs[2 * source][0, b], refs[2 * source + 1][0, b]
        rows, width = mine.shape
        out = refs[len(refs) - blocks + n]
        out[row : row + rows, cols[0] : cols[0] + width] = jnp.where(core == 0, mine, theirs)
        out[row : row + rows, cols[1] : cols[1] + width] = jnp.where(core == 0, theirs, mine)
    vectors, singles, wide = refs[2 * halves], refs[2 * halves + 1 : 2 * halves + 9], refs[2 * halves + 9]
    rows, per = singles[0].shape[0], wide.shape[0]
    turned = pltpu.roll(vectors[:8], lax.rem(D - pos_ref[0] * rows, D), 1)
    for n, single in enumerate(singles):
        single[...] = turned[n, :rows]
    at = pos_ref[0] * per
    turned = pltpu.roll(vectors[8:], lax.rem(D - lax.rem(at, D), D), 1)
    line = lax.broadcasted_iota(jnp.int32, turned.shape, 0) == at // D
    wide[...] = jnp.sum(jnp.where(line, turned, 0.0), axis=0)[:per]


def place(pos, sums, outs, after, vectors):
    places = [(k, b) + name for k, (_, _, names) in enumerate(sums) for b, name in enumerate(names)]
    rows = D // vectors.n_dp
    more = [(rows,)] * 8 + [(rows * FF // D,)]
    return small_call(
        functools.partial(place_kernel, places=places, blocks=len(outs), halves=len(sums)),
        "place",
        [pos],
        [x for mine, theirs, _ in sums for x in (mine, theirs)] + [vectors.total],
        [shape(dims, F32) for dims in more + outs],
        after,
    )


def count_rounds(labels, n_dp, window):
    hits = (labels[:, None] == jnp.arange(NTASK, dtype=jnp.int32)[None, :]).astype(jnp.int32)
    counts = [jnp.sum(hits, axis=0) * (2 * window)]
    bit = 1
    while bit < n_dp:
        masks = [bit] if 2 * bit >= n_dp else [bit, 2 * bit, 3 * bit]
        counts.append(counts[-1] + sum(swap_with(counts[-1], n_dp, (m, m)) for m in masks))
        bit *= 4
    return counts[1:]


def per_device(tokens, segments, labels, cotangent, w_qkv, b_query, b_value, w_out, b_out, gamma_one, beta_one, gamma_two, beta_two, w_up, b_up, w_down, b_down, *, n_dp):
    windows, window, width = tokens.shape
    pos = jnp.stack([lax.axis_index("dp"), lax.axis_index("group")]).astype(jnp.int32)
    x = tokens.reshape(window, width)
    cot = cotangent.reshape(window, width)
    counts = count_rounds(labels, n_dp, window)

    rows = D // n_dp
    moving = Transfers(pos, (counts[-1], labels), n_dp)

    down_names = [(0, b * rows, (0, HALF)) for b in range(4)]
    up_names = [(1, 0, (b * D, b * D + HALF)) for b in range(4)]
    first_names, last_names = [], []
    for b in range(3):
        for at in (b * D, b * D + LANES):
            first_names.append((2, 0, (at, at + 2 * LANES)))
        first_names.append((3, 0, (2 * b * LANES, (2 * b + 1) * LANES)))
        last_names.append((2, 0, (b * D + 4 * LANES, b * D + 5 * LANES)))
    chunks = {"D": down_names, "U": up_names, "F": first_names, "L": last_names}

    def begin(chunk, kind, own, other):
        moving.begin(kind, own, other, chunks[chunk], PLAN[chunk], chunk == "D")

    proj, in_one, att, probs, mid, in_two = forward(
        x, segments, gamma_one, beta_one, w_qkv, b_query, b_value, w_out, b_out, gamma_two, beta_two
    )
    act, slope, own, other = up(pos, in_two, cot, w_up, b_up, counts[:1])
    begin("D", "rows", own, other)
    after = []
    for step in SCHEDULE:
        if step == "hidden":
            gp, go, own, other, sum_up, sum_down = hidden(pos, counts[-1], labels, cot, in_two, slope, w_down)
            begin("U", "blocks", own, other)
            after = [gp]
        elif step == "middle":
            gm, gb, ga, sums_mid = middle_back(go, mid, gamma_two, gp, w_up, w_out, after)
            after = [ga]
        elif step == "attend first":
            first = attend_back(proj, ga, probs, 0, 4, after)
            after = [first]
        elif step == "first heads":
            own, other = first_heads(pos, in_one, first, att, gb, after)
            begin("F", "blocks", own, other)
            after = [own]
        elif step == "attend last":
            last = attend_back(proj, ga, probs, 4, 2, after)
            after = [last]
        elif step == "last heads":
            own, other = last_heads(pos, in_one, last, after)
            begin("L", "blocks", own, other)
            after = [own]
        elif step == "input":
            grad_tokens, vectors = input_back(
                x, gm, gamma_one, first, last, w_qkv, sums_mid, sum_down, sum_up, after
            )
            moving.vectors = Vectors(vectors, n_dp)
            after = [grad_tokens]
        elif step == "mix":
            mixed = mix(mid, act, w_down, b_down, after)
            after = [mixed]
        else:
            wanted = []
            for item in step:
                if item == "V":
                    wanted.append("vectors")
                else:
                    first_block = sum(count for count, _ in PLAN[item[0]][: int(item[1])])
                    wanted.append(chunks[item[0]][first_block])
            after = moving.tick(wanted, after)
    after = moving.finish(after)
    *singles, grad_b_up, grad_down, grad_up, grad_qkv, grad_out = place(
        pos, moving.mine, [(4 * rows, D), (rows, FF), (rows, 3 * D), (rows, D)], after, moving.vectors
    )
    query, value, gain_one, shift_one, gain_two, shift_two, out, bias_down = singles
    return (
        mixed.reshape(tokens.shape),
        grad_tokens.reshape(tokens.shape),
        grad_qkv,
        query,
        value,
        grad_out,
        out,
        gain_one,
        shift_one,
        gain_two,
        shift_two,
        grad_up,
        grad_b_up,
        grad_down,
        bias_down,
        counts[-1],
    )


def solution(mesh):
    split = P(("dp", "group"), None, None)
    return jax.shard_map(
        functools.partial(per_device, n_dp=mesh.shape["dp"]),
        mesh=mesh,
        in_specs=(split, P(("dp", "group"), None), P(("dp", "group")), split) + (P(),) * 13,
        out_specs=(split, split, P("dp", None), P("dp"), P("dp"), P("dp", None))
        + (P("dp"),) * 5
        + (P("dp", None), P("dp"), P("dp", None), P("dp"), P()),
        check_vma=False,
    )
```

profile of v0, /device:TPU:0, one launch (start us, length us, event | category | flops | bytes accessed | tf_op | source)
XLA Modules:
  0.0 210.0 jit_solution(4752526195247549697)
XLA Ops:
  1.3 4.0 %collective-permute-start.2 = (s32[3]{0:T(128)S(1)}, s32[3]{0:T(128)S(1)}, u32[]{:S(2)}, u32[]{:S(2)}) collective-permute-start(s32[3]{0:T(128)S(1)} %compare_select_fusion), channel_id=1, source_target_pairs={{0,6},{1,7},{2,4},{3,5},{4,2},{5,3},{6,0},{7,1},{8,14},{9,15},{10,... | collective-permute-start | bytes 44 | tf_op jit(solution)/shard_map/ppermute | solution.py:601
  6.0 22.2 %forward.1 = (bf16[3,1024,768]{2,1,0:T(8,128)(2,1)}, bf16[1024,768]{1,0:T(8,128)(2,1)}, bf16[1024,768]{1,0:T(8,128)(2,1)}, bf16[6,8,384,256]{3,2,1,0:T(8,128)(2,...) custom-call(bf16[1024,768]{1,0:T(8,128)(2,1)} %bitcast.30, s32[1,1024]{1,0:T(1,128)} %seg_ref.1, f32[768]{0:T(1024)} %refs_2_.5, ...), custom_call_target="tpu_custom_call" | custom-call | flops 96000000000 | bytes 24 | tf_op jit(solution)/shard_map/forward/pallas_call | solution.py:81
  28.2 4.1 %collective-permute-start.5 = (s32[3]{0:T(128)S(1)}, s32[3]{0:T(128)S(1)}, u32[]{:S(2)}, u32[]{:S(2)}) collective-permute-start(s32[3]{0:T(128)S(1)} %add_add_fusion.1.refs_5_), channel_id=1, source_target_pairs={{0,24},{1,25},{2,26},{3,27},{4,28},{5,29},{6,30},{7,31},{8,16},{9,... | collective-permute-start | bytes 44 | tf_op jit(solution)/shard_map/ppermute | solution.py:601
  32.9 16.7 %up_and_down_grad.1 = (bf16[1024,3072]{1,0:T(8,128)(2,1)}, bf16[1024,3072]{1,0:T(8,128)(2,1)}, f32[3072,384]{1,0:T(8,128)S(1)}, f32[3072,384]{1,0:T(8,128)}) custom-call(s32[2]{0:T(128)S(1)} %pad_add_fusion.refs_0_.pos_ref, bf16[1024,768]{1,0:T(8,128)(2,1)} %get-tuple-element.123.refs_1_.in_ref, bf16[1024,768]{1,0:T(8,128)(2,1)} %bitcast.28, ...), custom_call_target="tpu_custom_call" | custom-call | flops 64000000000 | bytes 16 | tf_op jit(solution)/shard_map/up_and_down_grad/pallas_call | solution.py:81
  49.7 16.6 %hidden_grad.1 = (bf16[1024,3072]{1,0:T(8,128)(2,1)S(1)}, bf16[1024,768]{1,0:T(8,128)(2,1)S(1)}, f32[4,768,384]{2,1,0:T(8,128)}, f32[4,768,384]{2,1,0:T(8,128)}, f32[4,1,768]{2,1,0:T(1,128)}, /*index=5*/f32[1,768]{1,0:T(1,128)}) custom-call(s32[2]{0:T(128)S(1)} %pad_add_fusion.refs_0_.pos_ref, s32[3]{0:T(128)S(1)} %add_add_fusion.counts_ref.refs_1_, ...), custom_call_target="tpu_custom_call" | custom-call | flops 56000000000 | bytes 14 | tf_op jit(solution)/shard_map/hidden_grad/pallas_call | solution.py:81
  66.3 2.6 %copy-done.3 = bf16[1024,3072]{1,0:T(8,128)(2,1)} copy-done((bf16[1024,3072]{1,0:T(8,128)(2,1)}, bf16[1024,3072]{1,0:T(8,128)(2,1)S(1)}, u32[]{:S(2)}) %copy-start.3) | copy-done | bytes 6291480
  69.4 2.3 %tick_1.1 = (f32[8,3,48,384]{3,2,1,0:T(8,128)}, f32[8,3,48,384]{3,2,1,0:T(8,128)S(1)}, f32[8,1,48,384]{3,2,1,0:T(8,128)S(1)}, f32[8,1,48,384]{3,2,1,0:T(8,128)S(1)}) custom-call(s32[2]{0:T(128)S(1)} %pad_add_fusion.refs_0_.pos_ref, s32[3]{0:T(128)S(1)} %add_add_fusion.counts_ref.refs_1_, s32[1]{0:T(128)} %copy.33.label_ref.refs_2_, ...), custom_call_target="tpu_custom_call" | custom-call | flops 1000000000 | bytes 1 | tf_op jit(solution)/shard_map/tick_1/pallas_call | solution.py:615
  71.7 1.4 collective-permute-start.8
  73.1 1.5 collective-permute-start.10
  74.6 12.2 %norm_two_back.1 = (f32[1024,768]{1,0:T(8,128)}, bf16[1024,768]{1,0:T(8,128)(2,1)}, bf16[1024,768]{1,0:T(8,128)(2,1)}, f32[3,768]{1,0:T(4,128)}) custom-call(bf16[1024,768]{1,0:T(8,128)(2,1)S(1)} %get-tuple-element.133.refs_0_, f32[1024,768]{1,0:T(8,128)} %get-tuple-element.122.refs_1_.refs_0_, f32[768]{0:T(1024)} %refs_2_.4, ...), custom_call_target="tpu_custom_call" | custom-call | flops 12000000000 | bytes 16 | tf_op jit(solution)/shard_map/norm_two_back/pallas_call | solution.py:81
  87.0 2.0 tick_2.1
  89.0 2.8 %collective-permute-start.9 = (f32[4,1,48,384]{3,2,1,0:T(8,128)S(1)}, f32[4,1,48,384]{3,2,1,0:T(8,128)S(1)}, u32[]{:S(2)}, u32[]{:S(2)}) collective-permute-start(f32[4,1,48,384]{3,2,1,0:T(8,128)S(1)} %get-tuple-element.137), channel_id=1, source_target_pairs={{0,16},{1,17},{2,18},{3,19},{4,20},{5,21},{6,22},{7,23},{8,24},{9,... | collective-permute-start | bytes 884744 | tf_op jit(solution)/shard_map/ppermute | solution.py:601
  91.8 1.5 collective-permute-start.12
  93.3 1.5 collective-permute-start.14
  94.8 9.4 %attend_back_first.1.refs_3_.refs_2_ = bf16[3,1024,512]{2,1,0:T(8,128)(2,1)S(1)} custom-call(bf16[3,1024,768]{2,1,0:T(8,128)(2,1)} %get-tuple-element.139.refs_0_.refs_1_.refs_2_, bf16[3,1024,768]{2,1,0:T(8,128)(2,1)} %get-tuple-element.139.refs_0_.refs_1_.refs_2_, bf16[3,1024,768]{2,1,0:T(8,128)(2,1)} %get-tuple-element.139.refs_0_.refs_1_.refs_2_, ...), custom_call_target="tpu_custom_call" | custom-call | flops 80000000000 | bytes 12 | tf_op jit(solution)/shard_map/attend_back_first/pallas_call | solution.py:81
  104.3 1.6 copy-done.1
  105.9 0.8 tick_3.1
  108.3 7.9 %first_heads_grad.1 = (f32[9,768,128]{2,1,0:T(8,128)}, f32[9,768,128]{2,1,0:T(8,128)}) custom-call(s32[2]{0:T(128)S(1)} %pad_add_fusion.refs_0_.pos_ref, bf16[1024,768]{1,0:T(8,128)(2,1)S(1)} %copy-done.7, bf16[3,1024,512]{2,1,0:T(8,128)(2,1)S(1)} %copy-done.2, bf16[1024,768]{1,0:T(8,128)(2,1)} %get-tuple-element.142.refs_3_, ...), custom_call_target="tpu_custom_call" | custom-call | bytes 10 | tf_op jit(solution)/shard_map/first_heads_grad/pallas_call | solution.py:81
  116.8 1.6 collective-permute-start.11
  119.7 6.0 %attend_back_last.1.refs_7_.refs_2_.refs_4_ = bf16[3,1024,256]{2,1,0:T(8,128)(2,1)S(1)} custom-call(bf16[3,1024,768]{2,1,0:T(8,128)(2,1)} %get-tuple-element.139.refs_0_.refs_1_.refs_2_, bf16[3,1024,768]{2,1,0:T(8,128)(2,1)} %get-tuple-element.139.refs_0_.refs_1_.refs_2_, bf16[3,1024,768]{2,1,0:T(8,128)(2,1)} %get-tuple-element.139.refs_0_.refs_1_.refs_2_, ...), custom_call_target="tpu_custom_call" | custom-call | flops 80000000000 | bytes 6 | tf_op jit(solution)/shard_map/attend_back_last/pallas_call | solution.py:81
  125.7 1.1 copy-done.5
  126.8 1.6 tick_6.1
  129.1 1.5 collective-permute-start.21
  130.6 3.4 %last_heads_grad.1 = (f32[3,768,128]{2,1,0:T(8,128)}, f32[3,768,128]{2,1,0:T(8,128)}) custom-call(s32[2]{0:T(128)S(1)} %pad_add_fusion.refs_0_.pos_ref, bf16[1024,768]{1,0:T(8,128)(2,1)S(1)} %copy-done.7, bf16[3,1024,256]{2,1,0:T(8,128)(2,1)S(1)} %copy-done.6, f32[1,1,48,384]{3,2,1,0:T(8,128)S(1)} %get-tuple-element.157.refs_3_), custom_call_target="tpu_custom_call" | custom-call | bytes 5 | tf_op jit(solution)/shard_map/last_heads_grad/pallas_call | solution.py:81
  133.9 1.5 collective-permute-start.19
  138.7 8.4 %norm_one_back.1 = (bf16[1024,768]{1,0:T(8,128)(2,1)}, f32[16,768]{1,0:T(8,128)}) custom-call(bf16[1024,768]{1,0:T(8,128)(2,1)} %bitcast.31, f32[1024,768]{1,0:T(8,128)} %get-tuple-element.167.refs_1_, f32[768]{0:T(1024)} %refs_2_.5, bf16[3,1024,512]{2,1,0:T(8,128)(2,1)S(1)} %copy-done.2, bf16[3,1024,256]{2,1,0:T(8,128)(2,1)S(1)} %copy-done.6, ...), custom_call_target="tpu_custom_call" | custom-call | flops 12000000000 | bytes 10 | tf_op jit(solution)/shard_map/norm_one_back/pallas_call | solution.py:81
  148.0 1.1 collective-permute-start.23
  149.1 1.2 collective-permute-done.24.refs_2_
  150.9 1.0 collective-permute-start.29
  151.8 1.5 collective-permute-done.17.refs_2_
  153.3 4.7 %collective-permute-done.23.refs_4_ = f32[2,1,48,384]{3,2,1,0:T(8,128)S(1)} collective-permute-done((f32[2,1,48,384]{3,2,1,0:T(8,128)S(1)}, f32[2,1,48,384]{3,2,1,0:T(8,128)S(1)}, u32[]{:S(2)}, u32[]{:S(2)}) %collective-permute-start.23) | collective-permute-done | bytes 147488 | tf_op jit(solution)/shard_map/ppermute | solution.py:601
  160.6 2.4 %collective-permute-start.27 = (f32[1,1,48,384]{3,2,1,0:T(8,128)S(1)}, f32[1,1,48,384]{3,2,1,0:T(8,128)S(1)}, u32[]{:S(2)}, u32[]{:S(2)}) collective-permute-start(f32[1,1,48,384]{3,2,1,0:T(8,128)S(1)} %get-tuple-element.182), channel_id=1, source_target_pairs={{0,16},{1,17},{2,18},{3,19},{4,20},{5,21},{6,22},{7,23},{8,24},{9,... | collective-permute-start | bytes 221192 | tf_op jit(solution)/shard_map/ppermute | solution.py:601
  163.0 1.5 collective-permute-start.32
  164.5 8.5 %mix.1.refs_9_ = bf16[1024,768]{1,0:T(8,128)(2,1)} custom-call(f32[1024,768]{1,0:T(8,128)} %get-tuple-element.122.refs_1_.refs_0_, bf16[1024,3072]{1,0:T(8,128)(2,1)} %get-tuple-element.124.refs_1_, bf16[3072,768]{1,0:T(8,128)(2,1)S(1)} %bitcast.24, f32[768]{0:T(1024)} %refs_3_.3, f32[4,6,48,128]{3,2,1,0:T(8,128)S(1)} %get-tuple-element.178.refs_4_), custom_call_target="tpu_custom_call" | custom-call | flops 80000000000 | bytes 10 | tf_op jit(solution)/shard_map/mix/pallas_call | solution.py:81
  173.0 2.3 %collective-permute-done.27.refs_4_ = f32[1,1,48,384]{3,2,1,0:T(8,128)S(1)} collective-permute-done((f32[1,1,48,384]{3,2,1,0:T(8,128)S(1)}, f32[1,1,48,384]{3,2,1,0:T(8,128)S(1)}, u32[]{:S(2)}, u32[]{:S(2)}) %collective-permute-start.27) | collective-permute-done | bytes 73760 | tf_op jit(solution)/shard_map/ppermute | solution.py:601
  176.7 1.4 collective-permute-start.35
  179.4 3.3 %collective-permute-done.36.refs_6_ = f32[16,768]{1,0:T(8,128)S(1)} collective-permute-done((f32[16,768]{1,0:T(8,128)S(1)}, f32[16,768]{1,0:T(8,128)S(1)}, u32[]{:S(2)}, u32[]{:S(2)}) %collective-permute-start.36) | collective-permute-done | bytes 49184 | tf_op jit(solution)/shard_map/ppermute | solution.py:601
  182.7 0.8 collective-permute-done.35.refs_4_
  185.5 1.8 collective-permute-start.42
  187.3 3.7 %collective-permute-done.42.refs_8_ = f32[16,768]{1,0:T(8,128)S(1)} collective-permute-done((f32[16,768]{1,0:T(8,128)S(1)}, f32[16,768]{1,0:T(8,128)S(1)}, u32[]{:S(2)}, u32[]{:S(2)}) %collective-permute-start.42) | collective-permute-done | bytes 49184 | tf_op jit(solution)/shard_map/ppermute | solution.py:601
  192.3 1.7 collective-permute-start.46
  194.0 1.3 collective-permute-start.44
  195.2 3.8 %collective-permute-done.46.refs_4_ = f32[16,768]{1,0:T(8,128)S(1)} collective-permute-done((f32[16,768]{1,0:T(8,128)S(1)}, f32[16,768]{1,0:T(8,128)S(1)}, u32[]{:S(2)}, u32[]{:S(2)}) %collective-permute-start.46) | collective-permute-done | bytes 49184 | tf_op jit(solution)/shard_map/ppermute | solution.py:601
  200.3 1.4 collective-permute-start.47
  202.2 2.8 %collective-permute-done.44.refs_2_ = f32[1,6,48,128]{3,2,1,0:T(8,128)S(1)} collective-permute-done((f32[1,6,48,128]{3,2,1,0:T(8,128)S(1)}, f32[1,6,48,128]{3,2,1,0:T(8,128)S(1)}, u32[]{:S(2)}, u32[]{:S(2)}) %collective-permute-start.44) | collective-permute-done | bytes 147488 | tf_op jit(solution)/shard_map/ppermute | solution.py:601
  205.0 0.8 collective-permute-done.47.refs_4_
  207.0 0.9 collective-permute-done.43.refs_10_
  208.2 1.8 place.1
  (128 shorter events, 22.5 us)
Async XLA Ops:
  1.3 26.8 %collective-permute-start.2 = (s32[3]{0:T(128)S(1)}, s32[3]{0:T(128)S(1)}, u32[]{:S(2)}, u32[]{:S(2)}) collective-permute-start(s32[3]{0:T(128)S(1)} %compare_select_fusion), channel_id=1, source_target_pairs={{0,6},{1,7},{2,4},{3,5},{4,2},{5,3},{6,0},{7,1},{8,14},{9,15},{10,... | collective-permute-start | bytes 44 | tf_op jit(solution)/shard_map/ppermute | solution.py:601
  5.3 22.9 %collective-permute-start.1 = (s32[3]{0:T(128)S(1)}, s32[3]{0:T(128)S(1)}, u32[]{:S(2)}, u32[]{:S(2)}) collective-permute-start(s32[3]{0:T(128)S(1)} %compare_select_fusion), channel_id=1, source_target_pairs={{0,4},{1,5},{2,6},{3,7},{4,0},{5,1},{6,2},{7,3},{8,12},{9,13},{10,... | collective-permute-start | bytes 44 | tf_op jit(solution)/shard_map/ppermute | solution.py:601
  5.8 22.4 %collective-permute-start = (s32[3]{0:T(128)S(1)}, s32[3]{0:T(128)S(1)}, u32[]{:S(2)}, u32[]{:S(2)}) collective-permute-start(s32[3]{0:T(128)S(1)} %compare_select_fusion), channel_id=1, source_target_pairs={{0,2},{1,3},{2,0},{3,1},{4,6},{5,7},{6,4},{7,5},{8,10},{9,11},{10,... | collective-permute-start | bytes 44 | tf_op jit(solution)/shard_map/ppermute | solution.py:601
  28.2 21.4 %collective-permute-start.5 = (s32[3]{0:T(128)S(1)}, s32[3]{0:T(128)S(1)}, u32[]{:S(2)}, u32[]{:S(2)}) collective-permute-start(s32[3]{0:T(128)S(1)} %add_add_fusion.1.refs_5_), channel_id=1, source_target_pairs={{0,24},{1,25},{2,26},{3,27},{4,28},{5,29},{6,30},{7,31},{8,16},{9,... | collective-permute-start | bytes 44 | tf_op jit(solution)/shard_map/ppermute | solution.py:601
  32.3 17.4 %collective-permute-start.4 = (s32[3]{0:T(128)S(1)}, s32[3]{0:T(128)S(1)}, u32[]{:S(2)}, u32[]{:S(2)}) collective-permute-start(s32[3]{0:T(128)S(1)} %add_add_fusion.1.refs_5_), channel_id=1, source_target_pairs={{0,16},{1,17},{2,18},{3,19},{4,20},{5,21},{6,22},{7,23},{8,24},{9,... | collective-permute-start | bytes 44 | tf_op jit(solution)/shard_map/ppermute | solution.py:601
  32.3 17.4 %collective-permute-start.3 = (s32[3]{0:T(128)S(1)}, s32[3]{0:T(128)S(1)}, u32[]{:S(2)}, u32[]{:S(2)}) collective-permute-start(s32[3]{0:T(128)S(1)} %add_add_fusion.1.refs_5_), channel_id=1, source_target_pairs={{0,8},{1,9},{2,10},{3,11},{4,12},{5,13},{6,14},{7,15},{8,0},{9,1},... | collective-permute-start | bytes 44 | tf_op jit(solution)/shard_map/ppermute | solution.py:601
  49.6 19.8 %collective-permute-start.7 = (f32[16,4,48,384]{3,2,1,0:T(8,128)}, f32[16,4,48,384]{3,2,1,0:T(8,128)S(1)}, u32[]{:S(2)}, u32[]{:S(2)}) collective-permute-start(f32[16,4,48,384]{3,2,1,0:T(8,128)} %bitcast.27), channel_id=1, source_target_pairs={{0,1},{1,0},{2,3},{3,2},{4,5},{5,4},{6,7},{7,6},{8,9},{9,8},{10,11... | collective-permute-start | bytes 14155784 | tf_op jit(solution)/shard_map/ppermute | solution.py:601
  68.9 17.9 %collective-permute-start.6 = (f32[4,16,48,384]{3,2,1,0:T(8,128)}, f32[4,16,48,384]{3,2,1,0:T(8,128)S(1)}, u32[]{:S(2)}, u32[]{:S(2)}) collective-permute-start(f32[4,16,48,384]{3,2,1,0:T(8,128)} %bitcast.26), channel_id=1, source_target_pairs={{0,1},{1,0},{2,3},{3,2},{4,5},{5,4},{6,7},{7,6},{8,9},{9,8},{10,11... | collective-permute-start | bytes 14155784 | tf_op jit(solution)/shard_map/ppermute | solution.py:601
  71.7 15.2 %collective-permute-start.8 = (f32[8,1,48,384]{3,2,1,0:T(8,128)S(1)}, f32[8,1,48,384]{3,2,1,0:T(8,128)S(1)}, u32[]{:S(2)}, u32[]{:S(2)}) collective-permute-start(f32[8,1,48,384]{3,2,1,0:T(8,128)S(1)} %get-tuple-element.132), channel_id=1, source_target_pairs={{0,8},{1,9},{2,10},{3,11},{4,12},{5,13},{6,14},{7,15},{8,0},{9,1},... | collective-permute-start | bytes 1769480 | tf_op jit(solution)/shard_map/ppermute | solution.py:601
  73.1 32.8 %collective-permute-start.10 = (f32[8,3,48,384]{3,2,1,0:T(8,128)}, f32[8,3,48,384]{3,2,1,0:T(8,128)S(1)}, u32[]{:S(2)}, u32[]{:S(2)}) collective-permute-start(f32[8,3,48,384]{3,2,1,0:T(8,128)} %get-tuple-element.134.refs_6_), channel_id=1, source_target_pairs={{0,4},{1,3},{2,6},{3,1},{4,0},{5,7},{6,2},{7,5},{8,12},{9,11},{10,... | collective-permute-start | bytes 5308424 | tf_op jit(solution)/shard_map/ppermute | solution.py:601
  89.0 27.1 %collective-permute-start.9 = (f32[4,1,48,384]{3,2,1,0:T(8,128)S(1)}, f32[4,1,48,384]{3,2,1,0:T(8,128)S(1)}, u32[]{:S(2)}, u32[]{:S(2)}) collective-permute-start(f32[4,1,48,384]{3,2,1,0:T(8,128)S(1)} %get-tuple-element.137), channel_id=1, source_target_pairs={{0,16},{1,17},{2,18},{3,19},{4,20},{5,21},{6,22},{7,23},{8,24},{9,... | collective-permute-start | bytes 884744 | tf_op jit(solution)/shard_map/ppermute | solution.py:601
  91.8 35.0 %collective-permute-start.12 = (f32[8,1,48,384]{3,2,1,0:T(8,128)}, f32[8,1,48,384]{3,2,1,0:T(8,128)}, u32[]{:S(2)}, u32[]{:S(2)}) collective-permute-start(f32[8,1,48,384]{3,2,1,0:T(8,128)} %get-tuple-element.150), channel_id=1, source_target_pairs={{0,8},{1,9},{2,10},{3,11},{4,12},{5,13},{6,14},{7,15},{8,0},{9,1},... | collective-permute-start | bytes 1769480 | tf_op jit(solution)/shard_map/ppermute | solution.py:601
  93.3 25.0 %collective-permute-start.14 = (f32[8,3,48,384]{3,2,1,0:T(8,128)S(1)}, f32[8,3,48,384]{3,2,1,0:T(8,128)S(1)}, u32[]{:S(2)}, u32[]{:S(2)}) collective-permute-start(f32[8,3,48,384]{3,2,1,0:T(8,128)S(1)} %get-tuple-element.141.refs_5_), channel_id=1, source_target_pairs={{0,2},{1,5},{2,0},{3,7},{4,6},{5,1},{6,4},{7,3},{8,10},{9,13},{10,... | collective-permute-start | bytes 5308424 | tf_op jit(solution)/shard_map/ppermute | solution.py:601
  106.7 30.0 %collective-permute-start.22 = (f32[4,3,48,384]{3,2,1,0:T(8,128)S(1)}, f32[4,3,48,384]{3,2,1,0:T(8,128)S(1)}, u32[]{:S(2)}, u32[]{:S(2)}) collective-permute-start(f32[4,3,48,384]{3,2,1,0:T(8,128)S(1)} %get-tuple-element.145.refs_5_), channel_id=1, source_target_pairs={{0,8},{1,9},{2,10},{3,11},{4,12},{5,13},{6,14},{7,15},{8,0},{9,1},... | collective-permute-start | bytes 2654216 | tf_op jit(solution)/shard_map/ppermute | solution.py:601
  116.8 10.0 %collective-permute-start.11 = (f32[2,1,48,384]{3,2,1,0:T(8,128)S(1)}, f32[2,1,48,384]{3,2,1,0:T(8,128)S(1)}, u32[]{:S(2)}, u32[]{:S(2)}) collective-permute-start(f32[2,1,48,384]{3,2,1,0:T(8,128)S(1)} %get-tuple-element.148.refs_3_), channel_id=1, source_target_pairs={{0,4},{1,3},{2,6},{3,1},{4,0},{5,7},{6,2},{7,5},{8,12},{9,11},{10,... | collective-permute-start | bytes 442376 | tf_op jit(solution)/shard_map/ppermute | solution.py:601
  118.4 8.4 %collective-permute-start.13 = (f32[9,16,48,128]{3,2,1,0:T(8,128)}, f32[9,16,48,128]{3,2,1,0:T(8,128)S(1)}, u32[]{:S(2)}, u32[]{:S(2)}) collective-permute-start(f32[9,16,48,128]{3,2,1,0:T(8,128)} %bitcast.10), channel_id=1, source_target_pairs={{0,1},{1,0},{2,3},{3,2},{4,5},{5,4},{6,7},{7,6},{8,9},{9,8},{10,11... | collective-permute-start | bytes 10616840 | tf_op jit(solution)/shard_map/ppermute | solution.py:601
  119.1 16.4 %collective-permute-start.16 = (f32[4,3,48,384]{3,2,1,0:T(8,128)S(1)}, f32[4,3,48,384]{3,2,1,0:T(8,128)S(1)}, u32[]{:S(2)}, u32[]{:S(2)}) collective-permute-start(f32[4,3,48,384]{3,2,1,0:T(8,128)S(1)} %get-tuple-element.153.refs_5_), channel_id=1, source_target_pairs={{0,4},{1,3},{2,6},{3,1},{4,0},{5,7},{6,2},{7,5},{8,12},{9,11},{10,... | collective-permute-start | bytes 2654216 | tf_op jit(solution)/shard_map/ppermute | solution.py:601
  128.5 9.2 %collective-permute-start.18 = (f32[4,1,48,384]{3,2,1,0:T(8,128)S(1)}, f32[4,1,48,384]{3,2,1,0:T(8,128)S(1)}, u32[]{:S(2)}, u32[]{:S(2)}) collective-permute-start(f32[4,1,48,384]{3,2,1,0:T(8,128)S(1)} %get-tuple-element.162), channel_id=1, source_target_pairs={{0,2},{1,5},{2,0},{3,7},{4,6},{5,1},{6,4},{7,3},{8,10},{9,13},{10,... | collective-permute-start | bytes 884744 | tf_op jit(solution)/shard_map/ppermute | solution.py:601
  129.1 8.3 %collective-permute-start.21 = (f32[1,1,48,384]{3,2,1,0:T(8,128)S(1)}, f32[1,1,48,384]{3,2,1,0:T(8,128)S(1)}, u32[]{:S(2)}, u32[]{:S(2)}) collective-permute-start(f32[1,1,48,384]{3,2,1,0:T(8,128)S(1)} %get-tuple-element.157.refs_3_), channel_id=1, source_target_pairs={{0,2},{1,5},{2,0},{3,7},{4,6},{5,1},{6,4},{7,3},{8,10},{9,13},{10,... | collective-permute-start | bytes 221192 | tf_op jit(solution)/shard_map/ppermute | solution.py:601
  133.9 13.2 %collective-permute-start.19 = (f32[8,3,48,128]{3,2,1,0:T(8,128)S(1)}, f32[8,3,48,128]{3,2,1,0:T(8,128)S(1)}, u32[]{:S(2)}, u32[]{:S(2)}) collective-permute-start(f32[8,3,48,128]{3,2,1,0:T(8,128)S(1)} %get-tuple-element.164), channel_id=1, source_target_pairs={{0,4},{1,3},{2,6},{3,1},{4,0},{5,7},{6,2},{7,5},{8,12},{9,11},{10,... | collective-permute-start | bytes 1769480 | tf_op jit(solution)/shard_map/ppermute | solution.py:601
  136.1 17.2 %collective-permute-start.17 = (f32[2,3,48,384]{3,2,1,0:T(8,128)S(1)}, f32[2,3,48,384]{3,2,1,0:T(8,128)S(1)}, u32[]{:S(2)}, u32[]{:S(2)}) collective-permute-start(f32[2,3,48,384]{3,2,1,0:T(8,128)S(1)} %get-tuple-element.160.refs_3_), channel_id=1, source_target_pairs={{0,8},{1,9},{2,10},{3,11},{4,12},{5,13},{6,14},{7,15},{8,0},{9,1},... | collective-permute-start | bytes 1327112 | tf_op jit(solution)/shard_map/ppermute | solution.py:601
  136.7 10.4 %collective-permute-start.20 = (f32[3,16,48,128]{3,2,1,0:T(8,128)S(1)}, f32[3,16,48,128]{3,2,1,0:T(8,128)S(1)}, u32[]{:S(2)}, u32[]{:S(2)}) collective-permute-start(f32[3,16,48,128]{3,2,1,0:T(8,128)S(1)} %bitcast.32), channel_id=1, source_target_pairs={{0,1},{1,0},{2,3},{3,2},{4,5},{5,4},{6,7},{7,6},{8,9},{9,8},{10,11... | collective-permute-start | bytes 3538952 | tf_op jit(solution)/shard_map/ppermute | solution.py:601
  137.4 23.2 %collective-permute-start.26 = (f32[2,3,48,384]{3,2,1,0:T(8,128)S(1)}, f32[2,3,48,384]{3,2,1,0:T(8,128)S(1)}, u32[]{:S(2)}, u32[]{:S(2)}) collective-permute-start(f32[2,3,48,384]{3,2,1,0:T(8,128)S(1)} %get-tuple-element.172.refs_9_), channel_id=1, source_target_pairs={{0,16},{1,17},{2,18},{3,19},{4,20},{5,21},{6,22},{7,23},{8,24},{9,... | collective-permute-start | bytes 1327112 | tf_op jit(solution)/shard_map/ppermute | solution.py:601
  137.7 21.5 %collective-permute-start.15 = (f32[8,6,48,128]{3,2,1,0:T(8,128)S(1)}, f32[8,6,48,128]{3,2,1,0:T(8,128)S(1)}, u32[]{:S(2)}, u32[]{:S(2)}) collective-permute-start(f32[8,6,48,128]{3,2,1,0:T(8,128)S(1)} %get-tuple-element.155), channel_id=1, source_target_pairs={{0,4},{1,3},{2,6},{3,1},{4,0},{5,7},{6,2},{7,5},{8,12},{9,11},{10,... | collective-permute-start | bytes 3538952 | tf_op jit(solution)/shard_map/ppermute | solution.py:601
  148.0 10.0 %collective-permute-start.23 = (f32[2,1,48,384]{3,2,1,0:T(8,128)S(1)}, f32[2,1,48,384]{3,2,1,0:T(8,128)S(1)}, u32[]{:S(2)}, u32[]{:S(2)}) collective-permute-start(f32[2,1,48,384]{3,2,1,0:T(8,128)S(1)} %get-tuple-element.175.refs_3_), channel_id=1, source_target_pairs={{0,4},{1,3},{2,6},{3,1},{4,0},{5,7},{6,2},{7,5},{8,12},{9,11},{10,... | collective-permute-start | bytes 442376 | tf_op jit(solution)/shard_map/ppermute | solution.py:601
  150.9 12.1 %collective-permute-start.29 = (f32[16,768]{1,0:T(8,128)S(1)}, f32[16,768]{1,0:T(8,128)S(1)}, u32[]{:S(2)}, u32[]{:S(2)}) collective-permute-start(f32[16,768]{1,0:T(8,128)S(1)} %tick_10.1.refs_5_.refs_7_), channel_id=1, source_target_pairs={{0,2},{1,3},{2,0},{3,1},{4,6},{5,7},{6,4},{7,5},{8,10},{9,11},{10,... | collective-permute-start | bytes 147464 | tf_op jit(solution)/shard_map/ppermute | solution.py:601
  153.3 22.0 %collective-permute-start.28 = (f32[4,3,48,128]{3,2,1,0:T(8,128)S(1)}, f32[4,3,48,128]{3,2,1,0:T(8,128)S(1)}, u32[]{:S(2)}, u32[]{:S(2)}) collective-permute-start(f32[4,3,48,128]{3,2,1,0:T(8,128)S(1)} %get-tuple-element.184), channel_id=1, source_target_pairs={{0,8},{1,9},{2,10},{3,11},{4,12},{5,13},{6,14},{7,15},{8,0},{9,1},... | collective-permute-start | bytes 884744 | tf_op jit(solution)/shard_map/ppermute | solution.py:601
  158.0 26.1 %collective-permute-start.38 = (f32[8,3,48,128]{3,2,1,0:T(8,128)S(1)}, f32[8,3,48,128]{3,2,1,0:T(8,128)S(1)}, u32[]{:S(2)}, u32[]{:S(2)}) collective-permute-start(f32[8,3,48,128]{3,2,1,0:T(8,128)S(1)} %get-tuple-element.196), channel_id=1, source_target_pairs={{0,2},{1,5},{2,0},{3,7},{4,6},{5,1},{6,4},{7,3},{8,10},{9,13},{10,... | collective-permute-start | bytes 1769480 | tf_op jit(solution)/shard_map/ppermute | solution.py:601
  159.2 18.8 %collective-permute-start.31 = (f32[1,3,48,384]{3,2,1,0:T(8,128)S(1)}, f32[1,3,48,384]{3,2,1,0:T(8,128)S(1)}, u32[]{:S(2)}, u32[]{:S(2)}) collective-permute-start(f32[1,3,48,384]{3,2,1,0:T(8,128)S(1)} %get-tuple-element.177.refs_3_), channel_id=1, source_target_pairs={{0,16},{1,17},{2,18},{3,19},{4,20},{5,21},{6,22},{7,23},{8,24},{9,... | collective-permute-start | bytes 663560 | tf_op jit(solution)/shard_map/ppermute | solution.py:601
  160.6 14.7 %collective-permute-start.27 = (f32[1,1,48,384]{3,2,1,0:T(8,128)S(1)}, f32[1,1,48,384]{3,2,1,0:T(8,128)S(1)}, u32[]{:S(2)}, u32[]{:S(2)}) collective-permute-start(f32[1,1,48,384]{3,2,1,0:T(8,128)S(1)} %get-tuple-element.182), channel_id=1, source_target_pairs={{0,16},{1,17},{2,18},{3,19},{4,20},{5,21},{6,22},{7,23},{8,24},{9,... | collective-permute-start | bytes 221192 | tf_op jit(solution)/shard_map/ppermute | solution.py:601
  163.0 15.7 %collective-permute-start.32 = (f32[4,6,48,128]{3,2,1,0:T(8,128)S(1)}, f32[4,6,48,128]{3,2,1,0:T(8,128)S(1)}, u32[]{:S(2)}, u32[]{:S(2)}) collective-permute-start(f32[4,6,48,128]{3,2,1,0:T(8,128)S(1)} %get-tuple-element.178.refs_4_), channel_id=1, source_target_pairs={{0,2},{1,5},{2,0},{3,7},{4,6},{5,1},{6,4},{7,3},{8,10},{9,13},{10,... | collective-permute-start | bytes 1769480 | tf_op jit(solution)/shard_map/ppermute | solution.py:601
  176.0 7.6 %collective-permute-start.34 = (f32[1,3,48,384]{3,2,1,0:T(8,128)S(1)}, f32[1,3,48,384]{3,2,1,0:T(8,128)S(1)}, u32[]{:S(2)}, u32[]{:S(2)}) collective-permute-start(f32[1,3,48,384]{3,2,1,0:T(8,128)S(1)} %get-tuple-element.188.refs_5_), channel_id=1, source_target_pairs={{0,2},{1,5},{2,0},{3,7},{4,6},{5,1},{6,4},{7,3},{8,10},{9,13},{10,... | collective-permute-start | bytes 663560 | tf_op jit(solution)/shard_map/ppermute | solution.py:601
  176.7 6.9 %collective-permute-start.35 = (f32[2,3,48,128]{3,2,1,0:T(8,128)S(1)}, f32[2,3,48,128]{3,2,1,0:T(8,128)S(1)}, u32[]{:S(2)}, u32[]{:S(2)}) collective-permute-start(f32[2,3,48,128]{3,2,1,0:T(8,128)S(1)} %get-tuple-element.192), channel_id=1, source_target_pairs={{0,2},{1,5},{2,0},{3,7},{4,6},{5,1},{6,4},{7,3},{8,10},{9,13},{10,... | collective-permute-start | bytes 442376 | tf_op jit(solution)/shard_map/ppermute | solution.py:601
  178.1 4.7 %collective-permute-start.36 = (f32[16,768]{1,0:T(8,128)S(1)}, f32[16,768]{1,0:T(8,128)S(1)}, u32[]{:S(2)}, u32[]{:S(2)}) collective-permute-start(f32[16,768]{1,0:T(8,128)S(1)} %get-tuple-element.193.refs_5_), channel_id=1, source_target_pairs={{0,4},{1,5},{2,6},{3,7},{4,0},{5,1},{6,2},{7,3},{8,12},{9,13},{10,... | collective-permute-start | bytes 147464 | tf_op jit(solution)/shard_map/ppermute | solution.py:601
  179.4 11.7 %collective-permute-start.41 = (f32[2,6,48,128]{3,2,1,0:T(8,128)S(1)}, f32[2,6,48,128]{3,2,1,0:T(8,128)S(1)}, u32[]{:S(2)}, u32[]{:S(2)}) collective-permute-start(f32[2,6,48,128]{3,2,1,0:T(8,128)S(1)} %get-tuple-element.202), channel_id=1, source_target_pairs={{0,8},{1,9},{2,10},{3,11},{4,12},{5,13},{6,14},{7,15},{8,0},{9,1},... | collective-permute-start | bytes 884744 | tf_op jit(solution)/shard_map/ppermute | solution.py:601
  184.8 6.8 %collective-permute-start.39 = (f32[4,3,48,128]{3,2,1,0:T(8,128)S(1)}, f32[4,3,48,128]{3,2,1,0:T(8,128)S(1)}, u32[]{:S(2)}, u32[]{:S(2)}) collective-permute-start(f32[4,3,48,128]{3,2,1,0:T(8,128)S(1)} %get-tuple-element.198.refs_9_), channel_id=1, source_target_pairs={{0,4},{1,3},{2,6},{3,1},{4,0},{5,7},{6,2},{7,5},{8,12},{9,11},{10,... | collective-permute-start | bytes 884744 | tf_op jit(solution)/shard_map/ppermute | solution.py:601
  185.5 5.5 %collective-permute-start.40 = (f32[1,3,48,128]{3,2,1,0:T(8,128)S(1)}, f32[1,3,48,128]{3,2,1,0:T(8,128)S(1)}, u32[]{:S(2)}, u32[]{:S(2)}) collective-permute-start(f32[1,3,48,128]{3,2,1,0:T(8,128)S(1)} %get-tuple-element.200), channel_id=1, source_target_pairs={{0,16},{1,17},{2,18},{3,19},{4,20},{5,21},{6,22},{7,23},{8,24},{9,... | collective-permute-start | bytes 221192 | tf_op jit(solution)/shard_map/ppermute | solution.py:601
  185.5 5.5 %collective-permute-start.42 = (f32[16,768]{1,0:T(8,128)S(1)}, f32[16,768]{1,0:T(8,128)S(1)}, u32[]{:S(2)}, u32[]{:S(2)}) collective-permute-start(f32[16,768]{1,0:T(8,128)S(1)} %get-tuple-element.203.refs_7_), channel_id=1, source_target_pairs={{0,8},{1,9},{2,10},{3,11},{4,12},{5,13},{6,14},{7,15},{8,0},{9,1},... | collective-permute-start | bytes 147464 | tf_op jit(solution)/shard_map/ppermute | solution.py:601
  192.2 7.6 %collective-permute-start.45 = (f32[2,3,48,128]{3,2,1,0:T(8,128)S(1)}, f32[2,3,48,128]{3,2,1,0:T(8,128)S(1)}, u32[]{:S(2)}, u32[]{:S(2)}) collective-permute-start(f32[2,3,48,128]{3,2,1,0:T(8,128)S(1)} %get-tuple-element.208.refs_5_), channel_id=1, source_target_pairs={{0,8},{1,9},{2,10},{3,11},{4,12},{5,13},{6,14},{7,15},{8,0},{9,1},... | collective-permute-start | bytes 442376 | tf_op jit(solution)/shard_map/ppermute | solution.py:601
  192.3 6.8 %collective-permute-start.46 = (f32[16,768]{1,0:T(8,128)S(1)}, f32[16,768]{1,0:T(8,128)S(1)}, u32[]{:S(2)}, u32[]{:S(2)}) collective-permute-start(f32[16,768]{1,0:T(8,128)S(1)} %get-tuple-element.209.refs_3_), channel_id=1, source_target_pairs={{0,16},{1,17},{2,18},{3,19},{4,20},{5,21},{6,22},{7,23},{8,24},{9,... | collective-permute-start | bytes 147464 | tf_op jit(solution)/shard_map/ppermute | solution.py:601
  194.0 11.0 %collective-permute-start.44 = (f32[1,6,48,128]{3,2,1,0:T(8,128)S(1)}, f32[1,6,48,128]{3,2,1,0:T(8,128)S(1)}, u32[]{:S(2)}, u32[]{:S(2)}) collective-permute-start(f32[1,6,48,128]{3,2,1,0:T(8,128)S(1)} %get-tuple-element.206), channel_id=1, source_target_pairs={{0,16},{1,17},{2,18},{3,19},{4,20},{5,21},{6,22},{7,23},{8,24},{9,... | collective-permute-start | bytes 442376 | tf_op jit(solution)/shard_map/ppermute | solution.py:601
  200.3 5.5 %collective-permute-start.47 = (f32[1,3,48,128]{3,2,1,0:T(8,128)S(1)}, f32[1,3,48,128]{3,2,1,0:T(8,128)S(1)}, u32[]{:S(2)}, u32[]{:S(2)}) collective-permute-start(f32[1,3,48,128]{3,2,1,0:T(8,128)S(1)} %get-tuple-element.211.refs_5_), channel_id=1, source_target_pairs={{0,16},{1,17},{2,18},{3,19},{4,20},{5,21},{6,22},{7,23},{8,24},{9,... | collective-permute-start | bytes 221192 | tf_op jit(solution)/shard_map/ppermute | solution.py:601
  201.7 4.8 %collective-permute-start.25 = (f32[1,1,48,384]{3,2,1,0:T(8,128)S(1)}, f32[1,1,48,384]{3,2,1,0:T(8,128)S(1)}, u32[]{:S(2)}, u32[]{:S(2)}) collective-permute-start(f32[1,1,48,384]{3,2,1,0:T(8,128)S(1)} %get-tuple-element.179.refs_1_), channel_id=1, source_target_pairs={{0,1},{1,0},{2,3},{3,2},{4,5},{5,4},{6,7},{7,6},{8,9},{9,8},{10,11... | collective-permute-start | bytes 221192 | tf_op jit(solution)/shard_map/ppermute | solution.py:601
  201.7 5.3 %collective-permute-start.30 = (f32[1,1,48,384]{3,2,1,0:T(8,128)S(1)}, f32[1,1,48,384]{3,2,1,0:T(8,128)S(1)}, u32[]{:S(2)}, u32[]{:S(2)}) collective-permute-start(f32[1,1,48,384]{3,2,1,0:T(8,128)S(1)} %get-tuple-element.185.refs_3_), channel_id=1, source_target_pairs={{0,1},{1,0},{2,3},{3,2},{4,5},{5,4},{6,7},{7,6},{8,9},{9,8},{10,11... | collective-permute-start | bytes 221192 | tf_op jit(solution)/shard_map/ppermute | solution.py:601
  202.2 4.8 %collective-permute-start.37 = (f32[1,3,48,384]{3,2,1,0:T(8,128)S(1)}, f32[1,3,48,384]{3,2,1,0:T(8,128)S(1)}, u32[]{:S(2)}, u32[]{:S(2)}) collective-permute-start(f32[1,3,48,384]{3,2,1,0:T(8,128)S(1)} %get-tuple-element.194.refs_3_.refs_7_), channel_id=1, source_target_pairs={{0,1},{1,0},{2,3},{3,2},{4,5},{5,4},{6,7},{7,6},{8,9},{9,8},{10,11... | collective-permute-start | bytes 663560 | tf_op jit(solution)/shard_map/ppermute | solution.py:601
  205.0 2.0 collective-permute-start.33
  206.3 1.9 collective-permute-start.48
  206.4 1.5 collective-permute-start.43
  (22 other events, 154.3 us)
where the time goes:
time: 210 us
  Pallas kernels  129 us (61%)
  starting transfers between devices  44 us (21%)
  waiting for transfers between devices  28.1 us (13%)
  local copies, waits for them, and re-layouts  6.86 us (3%)
    pallas_call x10, Pallas kernels, apply(): out = run(*args)  111 us
    ppermute x50, starting transfers between devices, swap_with(): return lax.ppermute(x, AXES, pairs)  44 us
    ppermute x50, waiting for transfers between devices, swap_with(): return lax.ppermute(x, AXES, pairs)  28.1 us
    pallas_call x20, Pallas kernels, small_call(): pl.pallas_call(body, in_specs=[SMEM] * len(scalars) + [vmem] * len(arrays...  18 us
    unnamed x40, local copies, waits for them, and re-layouts  6.86 us
  transfers between devices with their start and end apart: 50, of which 16 were waited for; matrix products, arithmetic and copies ran while one was open for 0% of the time, Pallas kernels for 60%

commit v1 on v0

--- a/solution.py
+++ b/solution.py
@@ -27,17 +27,56 @@
 NN = (((1,), (0,)), ((), ()))
 NT = (((1,), (1,)), ((), ()))
 TN = (((0,), (0,)), ((), ()))
-PLAN = {'D': [(3, ((1, 2, 3, 0), (0, 2, 3, 1))), (1, ((2, 3, 1, 0), (2, 3, 0, 1)))], 'U': [(3, ((0, 1, 2, 3), (1, 0, 2, 3))), (1, ((2, 0, 1, 3), (2, 1, 0, 3)))], 'F': [(3, ((1, 2, 0, 3), (0, 2, 1, 3))), (6, ((1, 0, 2, 3), (0, 1, 2, 3)))], 'L': [(3, ((0, 1, 2, 3), (1, 0, 2, 3)))]}
-SCHEDULE = ['hidden', ('D0', 'D1'), 'middle', ('U0', 'U1', 'D1'), 'attend first', ('D0',), 'first heads', ('D1',), ('U0',), 'attend last', ('D1', 'U1', 'F0', 'F1'), 'last heads', ('U0',), ('D0',), 'input', ('U1', 'F0', 'L0', 'D1'), ('V',), ('U0', 'U1'), ('F1',), 'mix', ('D0', 'U1', 'F0', 'V'), ('U0', 'F1'), ('D0', 'F0', 'V'), ('L0',), ('L0', 'V', 'F0', 'F1'), ('V', 'L0'), ('F1', 'L0')]
-SMALL_FLOPS = 1000000000
-SMALL_LIMIT = 20 * 2**20
-BIG = 1 << 40
-COST = {'first_heads_grad': 0, 'last_heads_grad': 0, 'attend_back_first': 20, 'attend_back_last': 20, 'norm_one_back': 3, 'mix': 20, 'norm_two_back': 3}
-FREE = {"hidden_grad": [6], "norm_two_back": [0, 3], "first_heads_grad": [1, 2], "last_heads_grad": [1, 2], "norm_one_back": [3, 4, 5], "mix": [2]}
-OUT = {"up_and_down_grad": [2], "hidden_grad": [0, 1], "attend_back_first": [0], "attend_back_last": [0]}
+PLAN = {'D': [(3, ((1, 2, 3, 0), (0, 2, 3, 1))), (1, ((2, 3, 1, 0), (2, 3, 0, 1)))],
+ 'U': [(3, ((0, 1, 2, 3), (1, 0, 2, 3))), (1, ((2, 0, 1, 3), (2, 1, 0, 3)))],
+ 'F': [(3, ((1, 2, 0, 3), (0, 2, 1, 3))), (6, ((1, 0, 2, 3), (0, 1, 2, 3)))],
+ 'L': [(3, ((0, 1, 2, 3), (1, 0, 2, 3)))]}
+SCHEDULE = ['hidden',
+ ('D0', 'D1'),
+ 'middle',
+ ('U0', 'U1', 'D1'),
+ 'attend first',
+ 'first heads',
+ ('D0',),
+ ('D1',),
+ ('U0',),
+ 'attend last',
+ ('D1', 'U1', 'F0', 'F1'),
+ 'last heads',
+ ('U0',),
+ ('D0',),
+ 'input',
+ ('U1', 'F0', 'L0', 'D1'),
+ ('V',),
+ ('U0', 'U1'),
+ ('F1',),
+ 'mix',
+ ('D0', 'U1', 'F0', 'V'),
+ ('U0', 'F1'),
+ ('D0', 'F0', 'V'),
+ ('L0',),
+ ('L0', 'V', 'F0', 'F1'),
+ ('V', 'L0'),
+ ('F1', 'L0')]
+COST = {'first_heads_grad': 0,
+ 'last_heads_grad': 0,
+ 'attend_back_first': 20,
+ 'attend_back_last': 20,
+ 'norm_one_back': 3,
+ 'mix': 20,
+ 'norm_two_back': 3,
+ 'hidden_grad': 60}
+FLOPS = 4e9
+TICK_FLOPS = 1000000000
+FREE = {'hidden_grad': [6],
+ 'norm_two_back': [0, 3],
+ 'first_heads_grad': [1, 2],
+ 'last_heads_grad': [1, 2],
+ 'norm_one_back': [3, 4, 5],
+ 'mix': [2]}
+OUT = {'up_and_down_grad': [2], 'hidden_grad': [0, 1], 'attend_back_first': [0], 'attend_back_last': [0]}
 VMEM_LIMIT = 34 * 2**20
-SCALE = 1
-FLOPS = 4e9
+TICK_LIMIT = 20 * 2**20
 
 
 def dot(a, b, dims=NN):
@@ -48,7 +87,7 @@
     return pltpu.with_memory_space_constraint(x, pltpu.HBM)
 
 
-def call(kernel, name, grid, in_specs, out_specs, out_shape, scratch=(), prefetch=0, us=3, after=0, free=(), limit=None):
+def call(kernel, name, grid, in_specs, out_specs, out_shape, scratch=(), prefetch=0, us=3, after=0, limit=None):
     in_specs = list(in_specs) + [pl.BlockSpec(memory_space=pl.ANY)] * after
     body = kernel
     if after:
@@ -70,13 +109,13 @@
         ),
         out_shape=made,
         compiler_params=pltpu.CompilerParams(vmem_limit_bytes=limit or VMEM_LIMIT),
-        cost_estimate=pl.CostEstimate(flops=int(COST.get(name, us) * FLOPS), bytes_accessed=int(us * SCALE), transcendentals=0),
+        cost_estimate=pl.CostEstimate(flops=int(COST.get(name, us) * FLOPS), bytes_accessed=us, transcendentals=0),
         name=name,
     )
 
     def apply(*args):
         last = len(args) - after
-        table = FREE.get(name, free)
+        table = FREE.get(name, ())
         args = [x if n < prefetch or n >= last or n in table else in_hbm(x) for n, x in enumerate(args)]
         out = run(*args)
         return out[0] if single else out
@@ -617,10 +656,10 @@
         in_specs=[SMEM] * len(scalars) + [vmem] * len(arrays) + [pl.BlockSpec(memory_space=pl.ANY)] * len(after),
         out_specs=[vmem] * len(outs),
         out_shape=outs,
-        compiler_params=pltpu.CompilerParams(vmem_limit_bytes=SMALL_LIMIT),
-        cost_estimate=pl.CostEstimate(flops=SMALL_FLOPS, bytes_accessed=1, transcendentals=0),
+        compiler_params=pltpu.CompilerParams(vmem_limit_bytes=TICK_LIMIT),
+        cost_estimate=pl.CostEstimate(flops=TICK_FLOPS, bytes_accessed=1, transcendentals=0),
         name=name,
-    )(*scalars, *[in_vmem(x) if x.size < BIG else x for x in arrays], *[in_hbm(a) if a.dtype == BF or a.ndim < 4 else a for a in after])
+    )(*scalars, *[in_vmem(x) for x in arrays], *[in_hbm(a) if a.dtype == BF or a.ndim < 4 else a for a in after])
 
 
 class Stream:

time: 210 us -> 209 us (level)
  starting transfers between devices: 44 us -> 48.1 us
  waiting for transfers between devices: 28.1 us -> 24.4 us
  local copies, waits for them, and re-layouts: 6.86 us -> 3.84 us
    ppermute x50, starting transfers between devices: 44 us -> 48.1 us  [swap_with(): return lax.ppermute(x, AXES, pairs)]
    ppermute x50, waiting for transfers between devices: 28.1 us -> 24.4 us  [swap_with(): return lax.ppermute(x, AXES, pairs)]
    unnamed x40 -> x36, local copies, waits for them, and re-layouts: 6.86 us -> 3.84 us
  transfers between devices with their start and end apart: 50 -> 50, of which waited for: 16 -> 16; matrix products, arithmetic and copies ran while one was open for 0% -> 0% of each run, Pallas kernels for 60% -> 61%
where the time goes in v1:
time: 209 us; the launch traced here: 208 us
  Pallas kernels  130 us (62%)
  starting transfers between devices  48.1 us (23%)
  waiting for transfers between devices  24.4 us (12%)
  local copies, waits for them, and re-layouts  3.84 us (2%)
    pallas_call x10, Pallas kernels, apply(): out = run(*args)  111 us
    ppermute x50, starting transfers between devices, swap_with(): return lax.ppermute(x, AXES, pairs)  48.1 us
    ppermute x50, waiting for transfers between devices, swap_with(): return lax.ppermute(x, AXES, pairs)  24.4 us
    pallas_call x20, Pallas kernels, small_call(): pl.pallas_call(body, in_specs=[SMEM] * len(scalars) + [vmem] * len(arrays...  18.9 us
  transfers between devices with their start and end apart: 50, of which 16 were waited for; matrix products, arithmetic and copies ran while one was open for 0% of the time, Pallas kernels for 61%

profile of v1, /device:TPU:0, one launch (start us, length us, event | category | flops | bytes accessed | tf_op | source)
XLA Modules:
  0.0 208.5 jit_solution(15980257265969838038)
XLA Ops:
  1.3 4.0 %collective-permute-start.2 = (s32[3]{0:T(128)S(1)}, s32[3]{0:T(128)S(1)}, u32[]{:S(2)}, u32[]{:S(2)}) collective-permute-start(s32[3]{0:T(128)S(1)} %compare_select_fusion), channel_id=1, source_target_pairs={{0,6},{1,7},{2,4},{3,5},{4,2},{5,3},{6,0},{7,1},{8,14},{9,15},{10,... | collective-permute-start | bytes 44 | tf_op jit(solution)/shard_map/ppermute | solution.py:640
  6.0 22.1 %forward.1 = (bf16[3,1024,768]{2,1,0:T(8,128)(2,1)}, bf16[1024,768]{1,0:T(8,128)(2,1)}, bf16[1024,768]{1,0:T(8,128)(2,1)}, bf16[6,8,384,256]{3,2,1,0:T(8,128)(2,...) custom-call(bf16[1024,768]{1,0:T(8,128)(2,1)} %bitcast.31, s32[1,1024]{1,0:T(1,128)} %seg_ref.1, f32[768]{0:T(1024)} %refs_2_.5, ...), custom_call_target="tpu_custom_call" | custom-call | flops 96000000000 | bytes 24 | tf_op jit(solution)/shard_map/forward/pallas_call | solution.py:120
  28.2 4.1 %collective-permute-start.5 = (s32[3]{0:T(128)S(1)}, s32[3]{0:T(128)S(1)}, u32[]{:S(2)}, u32[]{:S(2)}) collective-permute-start(s32[3]{0:T(128)S(1)} %add_add_fusion.1.refs_5_), channel_id=1, source_target_pairs={{0,24},{1,25},{2,26},{3,27},{4,28},{5,29},{6,30},{7,31},{8,16},{9,... | collective-permute-start | bytes 44 | tf_op jit(solution)/shard_map/ppermute | solution.py:640
  32.9 16.8 %up_and_down_grad.1 = (bf16[1024,3072]{1,0:T(8,128)(2,1)}, bf16[1024,3072]{1,0:T(8,128)(2,1)}, f32[3072,384]{1,0:T(8,128)S(1)}, f32[3072,384]{1,0:T(8,128)}) custom-call(s32[2]{0:T(128)S(1)} %pad_add_fusion.refs_0_.pos_ref, bf16[1024,768]{1,0:T(8,128)(2,1)} %get-tuple-element.123.refs_1_.in_ref, bf16[1024,768]{1,0:T(8,128)(2,1)} %bitcast.29, ...), custom_call_target="tpu_custom_call" | custom-call | flops 64000000000 | bytes 16 | tf_op jit(solution)/shard_map/up_and_down_grad/pallas_call | solution.py:120
  49.7 16.6 %hidden_grad.1 = (bf16[1024,3072]{1,0:T(8,128)(2,1)S(1)}, bf16[1024,768]{1,0:T(8,128)(2,1)S(1)}, f32[4,768,384]{2,1,0:T(8,128)}, f32[4,768,384]{2,1,0:T(8,128)}, f32[4,1,768]{2,1,0:T(1,128)}, /*index=5*/f32[1,768]{1,0:T(1,128)}) custom-call(s32[2]{0:T(128)S(1)} %pad_add_fusion.refs_0_.pos_ref, s32[3]{0:T(128)S(1)} %add_add_fusion.counts_ref.refs_1_, ...), custom_call_target="tpu_custom_call" | custom-call | flops 240000008192 | bytes 14 | tf_op jit(solution)/shard_map/hidden_grad/pallas_call | solution.py:120
  66.3 2.6 %copy-done.1 = bf16[1024,3072]{1,0:T(8,128)(2,1)} copy-done((bf16[1024,3072]{1,0:T(8,128)(2,1)}, bf16[1024,3072]{1,0:T(8,128)(2,1)S(1)}, u32[]{:S(2)}) %copy-start.1) | copy-done | bytes 6291480
  69.4 3.2 %tick_1.1 = (f32[8,3,48,384]{3,2,1,0:T(8,128)S(1)}, f32[8,3,48,384]{3,2,1,0:T(8,128)S(1)}, f32[8,1,48,384]{3,2,1,0:T(8,128)S(1)}, f32[8,1,48,384]{3,2,1,0:T(8,128)S(1)}) custom-call(s32[2]{0:T(128)S(1)} %pad_add_fusion.refs_0_.pos_ref, s32[3]{0:T(128)S(1)} %add_add_fusion.counts_ref.refs_1_, s32[1]{0:T(128)} %copy.33.label_ref.refs_2_, ...), custom_call_target="tpu_custom_call" | custom-call | flops 1000000000 | bytes 1 | tf_op jit(solution)/shard_map/tick_1/pallas_call | solution.py:654
  72.6 1.5 collective-permute-start.8
  74.1 1.5 collective-permute-start.10
  75.6 12.2 %norm_two_back.1 = (f32[1024,768]{1,0:T(8,128)}, bf16[1024,768]{1,0:T(8,128)(2,1)}, bf16[1024,768]{1,0:T(8,128)(2,1)}, f32[3,768]{1,0:T(4,128)}) custom-call(bf16[1024,768]{1,0:T(8,128)(2,1)S(1)} %get-tuple-element.133.refs_0_, f32[1024,768]{1,0:T(8,128)} %get-tuple-element.122.refs_1_.refs_0_, f32[768]{0:T(1024)} %refs_2_.4, ...), custom_call_target="tpu_custom_call" | custom-call | flops 12000000000 | bytes 16 | tf_op jit(solution)/shard_map/norm_two_back/pallas_call | solution.py:120
  87.9 2.0 tick_2.1
  90.0 2.9 %collective-permute-start.9 = (f32[4,1,48,384]{3,2,1,0:T(8,128)S(1)}, f32[4,1,48,384]{3,2,1,0:T(8,128)S(1)}, u32[]{:S(2)}, u32[]{:S(2)}) collective-permute-start(f32[4,1,48,384]{3,2,1,0:T(8,128)S(1)} %get-tuple-element.137), channel_id=1, source_target_pairs={{0,16},{1,17},{2,18},{3,19},{4,20},{5,21},{6,22},{7,23},{8,24},{9,... | collective-permute-start | bytes 884744 | tf_op jit(solution)/shard_map/ppermute | solution.py:640
  92.8 1.4 collective-permute-start.12
  94.3 1.5 collective-permute-start.14
  95.8 9.5 %attend_back_first.1.refs_2_.refs_5_.refs_3_ = bf16[3,1024,512]{2,1,0:T(8,128)(2,1)S(1)} custom-call(bf16[3,1024,768]{2,1,0:T(8,128)(2,1)} %get-tuple-element.140.refs_0_.refs_1_.refs_2_, bf16[3,1024,768]{2,1,0:T(8,128)(2,1)} %get-tuple-element.140.refs_0_.refs_1_.refs_2_, bf16[3,1024,768]{2,1,0:T(8,128)(2,1)} %get-tuple-element.140.refs_0_.refs_1_.refs_2_, ...), custom_call_target="tpu_custom_call" | custom-call | flops 80000000000 | bytes 12 | tf_op jit(solution)/shard_map/attend_back_first/pallas_call | solution.py:120
  105.3 7.9 %first_heads_grad.1 = (f32[9,768,128]{2,1,0:T(8,128)}, f32[9,768,128]{2,1,0:T(8,128)}) custom-call(s32[2]{0:T(128)S(1)} %pad_add_fusion.refs_0_.pos_ref, bf16[1024,768]{1,0:T(8,128)(2,1)S(1)} %copy-done.5, bf16[3,1024,512]{2,1,0:T(8,128)(2,1)S(1)} %attend_back_first.1.refs_2_.refs_5_.refs_3_, bf16[1024,768]{1,0:T(8,128)(2,1)} %get-tuple-element.143.refs_3_, ...), custom_call_target="tpu_custom_call" | custom-call | bytes 10 | tf_op jit(solution)/shard_map/first_heads_grad/pallas_call | solution.py:120
  115.2 1.3 collective-permute-start.11
  117.5 1.6 collective-permute-start.16
  119.1 6.0 %attend_back_last.1.refs_7_.refs_2_.refs_4_ = bf16[3,1024,256]{2,1,0:T(8,128)(2,1)S(1)} custom-call(bf16[3,1024,768]{2,1,0:T(8,128)(2,1)} %get-tuple-element.140.refs_0_.refs_1_.refs_2_, bf16[3,1024,768]{2,1,0:T(8,128)(2,1)} %get-tuple-element.140.refs_0_.refs_1_.refs_2_, bf16[3,1024,768]{2,1,0:T(8,128)(2,1)} %get-tuple-element.140.refs_0_.refs_1_.refs_2_, ...), custom_call_target="tpu_custom_call" | custom-call | flops 80000000000 | bytes 6 | tf_op jit(solution)/shard_map/attend_back_last/pallas_call | solution.py:120
  125.1 1.1 copy-done.3
  126.3 1.6 tick_6.1
  127.9 1.6 collective-permute-start.18
  130.0 3.4 %last_heads_grad.1 = (f32[3,768,128]{2,1,0:T(8,128)}, f32[3,768,128]{2,1,0:T(8,128)}) custom-call(s32[2]{0:T(128)S(1)} %pad_add_fusion.refs_0_.pos_ref, bf16[1024,768]{1,0:T(8,128)(2,1)S(1)} %copy-done.5, bf16[3,1024,256]{2,1,0:T(8,128)(2,1)S(1)} %copy-done.4, f32[1,1,48,384]{3,2,1,0:T(8,128)S(1)} %get-tuple-element.157.refs_3_), custom_call_target="tpu_custom_call" | custom-call | bytes 5 | tf_op jit(solution)/shard_map/last_heads_grad/pallas_call | solution.py:120
  134.6 1.5 collective-permute-start.17
  137.2 1.6 collective-permute-start.15
  138.8 8.4 %norm_one_back.1 = (bf16[1024,768]{1,0:T(8,128)(2,1)}, f32[16,768]{1,0:T(8,128)}) custom-call(bf16[1024,768]{1,0:T(8,128)(2,1)} %bitcast.32, f32[1024,768]{1,0:T(8,128)} %get-tuple-element.167.refs_1_, f32[768]{0:T(1024)} %refs_2_.5, bf16[3,1024,512]{2,1,0:T(8,128)(2,1)S(1)} %attend_back_first.1.refs_2_.refs_5_.refs_3_, bf16[3,1024,256]{2,1,0:T(8,128)(2,1)S(1)} %copy-done.4, ...), custom_call_target="tpu_custom_call" | custom-call | flops 12000000000 | bytes 10 | tf_op jit(solution)/shard_map/norm_one_back/pallas_call | solution.py:120
  148.1 1.2 collective-permute-start.23
  149.3 1.2 collective-permute-done.24.refs_2_
  151.1 1.5 collective-permute-start.29
  152.9 4.6 %collective-permute-done.23.refs_4_ = f32[2,1,48,384]{3,2,1,0:T(8,128)S(1)} collective-permute-done((f32[2,1,48,384]{3,2,1,0:T(8,128)S(1)}, f32[2,1,48,384]{3,2,1,0:T(8,128)S(1)}, u32[]{:S(2)}, u32[]{:S(2)}) %collective-permute-start.23) | collective-permute-done | bytes 147488 | tf_op jit(solution)/shard_map/ppermute | solution.py:640
  157.5 1.5 collective-permute-start.38
  159.6 1.2 collective-permute-start.31
  161.5 1.9 collective-permute-start.27
  163.9 8.5 %mix.1.refs_9_ = bf16[1024,768]{1,0:T(8,128)(2,1)} custom-call(f32[1024,768]{1,0:T(8,128)} %get-tuple-element.122.refs_1_.refs_0_, bf16[1024,3072]{1,0:T(8,128)(2,1)} %get-tuple-element.124.refs_1_, bf16[3072,768]{1,0:T(8,128)(2,1)S(1)} %bitcast.24, f32[768]{0:T(1024)} %refs_3_.3, f32[4,6,48,128]{3,2,1,0:T(8,128)S(1)} %get-tuple-element.178.refs_4_), custom_call_target="tpu_custom_call" | custom-call | flops 80000000000 | bytes 10 | tf_op jit(solution)/shard_map/mix/pallas_call | solution.py:120
  172.5 1.4 collective-permute-done.27.refs_4_
  174.5 1.5 collective-permute-start.34
  176.6 1.4 collective-permute-start.36
  178.7 2.0 collective-permute-done.36.refs_6_
  180.7 1.4 collective-permute-done.35.refs_4_
  183.4 1.4 collective-permute-start.39
  184.8 1.2 collective-permute-start.42
  186.0 2.9 %collective-permute-done.42.refs_8_ = f32[16,768]{1,0:T(8,128)S(1)} collective-permute-done((f32[16,768]{1,0:T(8,128)S(1)}, f32[16,768]{1,0:T(8,128)S(1)}, u32[]{:S(2)}, u32[]{:S(2)}) %collective-permute-start.42) | collective-permute-done | bytes 49184 | tf_op jit(solution)/shard_map/ppermute | solution.py:640
  188.9 1.2 collective-permute-done.40.refs_4_
  190.8 2.2 %collective-permute-start.46 = (f32[16,768]{1,0:T(8,128)S(1)}, f32[16,768]{1,0:T(8,128)S(1)}, u32[]{:S(2)}, u32[]{:S(2)}) collective-permute-start(f32[16,768]{1,0:T(8,128)S(1)} %get-tuple-element.209.refs_3_), channel_id=1, source_target_pairs={{0,16},{1,17},{2,18},{3,19},{4,20},{5,21},{6,22},{7,23},{8,24},{9,... | collective-permute-start | bytes 147464 | tf_op jit(solution)/shard_map/ppermute | solution.py:640
  193.8 3.8 %collective-permute-done.46.refs_4_ = f32[16,768]{1,0:T(8,128)S(1)} collective-permute-done((f32[16,768]{1,0:T(8,128)S(1)}, f32[16,768]{1,0:T(8,128)S(1)}, u32[]{:S(2)}, u32[]{:S(2)}) %collective-permute-start.46) | collective-permute-done | bytes 49184 | tf_op jit(solution)/shard_map/ppermute | solution.py:640
  198.2 1.6 collective-permute-start.47
  200.4 3.0 %collective-permute-done.44.refs_2_ = f32[1,6,48,128]{3,2,1,0:T(8,128)S(1)} collective-permute-done((f32[1,6,48,128]{3,2,1,0:T(8,128)S(1)}, f32[1,6,48,128]{3,2,1,0:T(8,128)S(1)}, u32[]{:S(2)}, u32[]{:S(2)}) %collective-permute-start.44) | collective-permute-done | bytes 147488 | tf_op jit(solution)/shard_map/ppermute | solution.py:640
  206.6 1.8 place.1
  (124 shorter events, 20.4 us)
Async XLA Ops:
  1.3 26.8 %collective-permute-start.2 = (s32[3]{0:T(128)S(1)}, s32[3]{0:T(128)S(1)}, u32[]{:S(2)}, u32[]{:S(2)}) collective-permute-start(s32[3]{0:T(128)S(1)} %compare_select_fusion), channel_id=1, source_target_pairs={{0,6},{1,7},{2,4},{3,5},{4,2},{5,3},{6,0},{7,1},{8,14},{9,15},{10,... | collective-permute-start | bytes 44 | tf_op jit(solution)/shard_map/ppermute | solution.py:640
  5.3 22.9 %collective-permute-start.1 = (s32[3]{0:T(128)S(1)}, s32[3]{0:T(128)S(1)}, u32[]{:S(2)}, u32[]{:S(2)}) collective-permute-start(s32[3]{0:T(128)S(1)} %compare_select_fusion), channel_id=1, source_target_pairs={{0,4},{1,5},{2,6},{3,7},{4,0},{5,1},{6,2},{7,3},{8,12},{9,13},{10,... | collective-permute-start | bytes 44 | tf_op jit(solution)/shard_map/ppermute | solution.py:640
  5.8 22.4 %collective-permute-start = (s32[3]{0:T(128)S(1)}, s32[3]{0:T(128)S(1)}, u32[]{:S(2)}, u32[]{:S(2)}) collective-permute-start(s32[3]{0:T(128)S(1)} %compare_select_fusion), channel_id=1, source_target_pairs={{0,2},{1,3},{2,0},{3,1},{4,6},{5,7},{6,4},{7,5},{8,10},{9,11},{10,... | collective-permute-start | bytes 44 | tf_op jit(solution)/shard_map/ppermute | solution.py:640
  28.2 21.5 %collective-permute-start.5 = (s32[3]{0:T(128)S(1)}, s32[3]{0:T(128)S(1)}, u32[]{:S(2)}, u32[]{:S(2)}) collective-permute-start(s32[3]{0:T(128)S(1)} %add_add_fusion.1.refs_5_), channel_id=1, source_target_pairs={{0,24},{1,25},{2,26},{3,27},{4,28},{5,29},{6,30},{7,31},{8,16},{9,... | collective-permute-start | bytes 44 | tf_op jit(solution)/shard_map/ppermute | solution.py:640
  32.2 17.4 %collective-permute-start.4 = (s32[3]{0:T(128)S(1)}, s32[3]{0:T(128)S(1)}, u32[]{:S(2)}, u32[]{:S(2)}) collective-permute-start(s32[3]{0:T(128)S(1)} %add_add_fusion.1.refs_5_), channel_id=1, source_target_pairs={{0,16},{1,17},{2,18},{3,19},{4,20},{5,21},{6,22},{7,23},{8,24},{9,... | collective-permute-start | bytes 44 | tf_op jit(solution)/shard_map/ppermute | solution.py:640
  32.2 17.4 %collective-permute-start.3 = (s32[3]{0:T(128)S(1)}, s32[3]{0:T(128)S(1)}, u32[]{:S(2)}, u32[]{:S(2)}) collective-permute-start(s32[3]{0:T(128)S(1)} %add_add_fusion.1.refs_5_), channel_id=1, source_target_pairs={{0,8},{1,9},{2,10},{3,11},{4,12},{5,13},{6,14},{7,15},{8,0},{9,1},... | collective-permute-start | bytes 44 | tf_op jit(solution)/shard_map/ppermute | solution.py:640
  49.6 19.8 %collective-permute-start.7 = (f32[16,4,48,384]{3,2,1,0:T(8,128)}, f32[16,4,48,384]{3,2,1,0:T(8,128)}, u32[]{:S(2)}, u32[]{:S(2)}) collective-permute-start(f32[16,4,48,384]{3,2,1,0:T(8,128)} %bitcast.27), channel_id=1, source_target_pairs={{0,1},{1,0},{2,3},{3,2},{4,5},{5,4},{6,7},{7,6},{8,9},{9,8},{10,11... | collective-permute-start | bytes 14155784 | tf_op jit(solution)/shard_map/ppermute | solution.py:640
  68.9 18.9 %collective-permute-start.6 = (f32[4,16,48,384]{3,2,1,0:T(8,128)}, f32[4,16,48,384]{3,2,1,0:T(8,128)S(1)}, u32[]{:S(2)}, u32[]{:S(2)}) collective-permute-start(f32[4,16,48,384]{3,2,1,0:T(8,128)} %bitcast.26), channel_id=1, source_target_pairs={{0,1},{1,0},{2,3},{3,2},{4,5},{5,4},{6,7},{7,6},{8,9},{9,8},{10,11... | collective-permute-start | bytes 14155784 | tf_op jit(solution)/shard_map/ppermute | solution.py:640
  72.6 15.3 %collective-permute-start.8 = (f32[8,1,48,384]{3,2,1,0:T(8,128)S(1)}, f32[8,1,48,384]{3,2,1,0:T(8,128)S(1)}, u32[]{:S(2)}, u32[]{:S(2)}) collective-permute-start(f32[8,1,48,384]{3,2,1,0:T(8,128)S(1)} %get-tuple-element.132), channel_id=1, source_target_pairs={{0,8},{1,9},{2,10},{3,11},{4,12},{5,13},{6,14},{7,15},{8,0},{9,1},... | collective-permute-start | bytes 1769480 | tf_op jit(solution)/shard_map/ppermute | solution.py:640
  74.1 39.2 %collective-permute-start.10 = (f32[8,3,48,384]{3,2,1,0:T(8,128)S(1)}, f32[8,3,48,384]{3,2,1,0:T(8,128)S(1)}, u32[]{:S(2)}, u32[]{:S(2)}) collective-permute-start(f32[8,3,48,384]{3,2,1,0:T(8,128)S(1)} %get-tuple-element.134.refs_6_), channel_id=1, source_target_pairs={{0,4},{1,3},{2,6},{3,1},{4,0},{5,7},{6,2},{7,5},{8,12},{9,11},{10,... | collective-permute-start | bytes 5308424 | tf_op jit(solution)/shard_map/ppermute | solution.py:640
  90.0 24.7 %collective-permute-start.9 = (f32[4,1,48,384]{3,2,1,0:T(8,128)S(1)}, f32[4,1,48,384]{3,2,1,0:T(8,128)S(1)}, u32[]{:S(2)}, u32[]{:S(2)}) collective-permute-start(f32[4,1,48,384]{3,2,1,0:T(8,128)S(1)} %get-tuple-element.137), channel_id=1, source_target_pairs={{0,16},{1,17},{2,18},{3,19},{4,20},{5,21},{6,22},{7,23},{8,24},{9,... | collective-permute-start | bytes 884744 | tf_op jit(solution)/shard_map/ppermute | solution.py:640
  92.8 33.4 %collective-permute-start.12 = (f32[8,1,48,384]{3,2,1,0:T(8,128)}, f32[8,1,48,384]{3,2,1,0:T(8,128)}, u32[]{:S(2)}, u32[]{:S(2)}) collective-permute-start(f32[8,1,48,384]{3,2,1,0:T(8,128)} %get-tuple-element.150), channel_id=1, source_target_pairs={{0,8},{1,9},{2,10},{3,11},{4,12},{5,13},{6,14},{7,15},{8,0},{9,1},... | collective-permute-start | bytes 1769480 | tf_op jit(solution)/shard_map/ppermute | solution.py:640
  94.3 22.5 %collective-permute-start.14 = (f32[8,3,48,384]{3,2,1,0:T(8,128)S(1)}, f32[8,3,48,384]{3,2,1,0:T(8,128)S(1)}, u32[]{:S(2)}, u32[]{:S(2)}) collective-permute-start(f32[8,3,48,384]{3,2,1,0:T(8,128)S(1)} %get-tuple-element.142.refs_5_), channel_id=1, source_target_pairs={{0,2},{1,5},{2,0},{3,7},{4,6},{5,1},{6,4},{7,3},{8,10},{9,13},{10,... | collective-permute-start | bytes 5308424 | tf_op jit(solution)/shard_map/ppermute | solution.py:640
  113.2 13.0 %collective-permute-start.13 = (f32[9,16,48,128]{3,2,1,0:T(8,128)}, f32[9,16,48,128]{3,2,1,0:T(8,128)S(1)}, u32[]{:S(2)}, u32[]{:S(2)}) collective-permute-start(f32[9,16,48,128]{3,2,1,0:T(8,128)} %bitcast.28), channel_id=1, source_target_pairs={{0,1},{1,0},{2,3},{3,2},{4,5},{5,4},{6,7},{7,6},{8,9},{9,8},{10,11... | collective-permute-start | bytes 10616840 | tf_op jit(solution)/shard_map/ppermute | solution.py:640
  114.0 22.5 %collective-permute-start.22 = (f32[4,3,48,384]{3,2,1,0:T(8,128)S(1)}, f32[4,3,48,384]{3,2,1,0:T(8,128)S(1)}, u32[]{:S(2)}, u32[]{:S(2)}) collective-permute-start(f32[4,3,48,384]{3,2,1,0:T(8,128)S(1)} %get-tuple-element.146.refs_3_), channel_id=1, source_target_pairs={{0,8},{1,9},{2,10},{3,11},{4,12},{5,13},{6,14},{7,15},{8,0},{9,1},... | collective-permute-start | bytes 2654216 | tf_op jit(solution)/shard_map/ppermute | solution.py:640
  115.2 11.0 %collective-permute-start.11 = (f32[2,1,48,384]{3,2,1,0:T(8,128)S(1)}, f32[2,1,48,384]{3,2,1,0:T(8,128)S(1)}, u32[]{:S(2)}, u32[]{:S(2)}) collective-permute-start(f32[2,1,48,384]{3,2,1,0:T(8,128)S(1)} %get-tuple-element.148.refs_3_), channel_id=1, source_target_pairs={{0,4},{1,3},{2,6},{3,1},{4,0},{5,7},{6,2},{7,5},{8,12},{9,11},{10,... | collective-permute-start | bytes 442376 | tf_op jit(solution)/shard_map/ppermute | solution.py:640
  117.5 16.4 %collective-permute-start.16 = (f32[4,3,48,384]{3,2,1,0:T(8,128)S(1)}, f32[4,3,48,384]{3,2,1,0:T(8,128)S(1)}, u32[]{:S(2)}, u32[]{:S(2)}) collective-permute-start(f32[4,3,48,384]{3,2,1,0:T(8,128)S(1)} %get-tuple-element.153.refs_5_), channel_id=1, source_target_pairs={{0,4},{1,3},{2,6},{3,1},{4,0},{5,7},{6,2},{7,5},{8,12},{9,11},{10,... | collective-permute-start | bytes 2654216 | tf_op jit(solution)/shard_map/ppermute | solution.py:640
  127.9 9.3 %collective-permute-start.18 = (f32[4,1,48,384]{3,2,1,0:T(8,128)S(1)}, f32[4,1,48,384]{3,2,1,0:T(8,128)S(1)}, u32[]{:S(2)}, u32[]{:S(2)}) collective-permute-start(f32[4,1,48,384]{3,2,1,0:T(8,128)S(1)} %get-tuple-element.162), channel_id=1, source_target_pairs={{0,2},{1,5},{2,0},{3,7},{4,6},{5,1},{6,4},{7,3},{8,10},{9,13},{10,... | collective-permute-start | bytes 884744 | tf_op jit(solution)/shard_map/ppermute | solution.py:640
  129.5 7.6 %collective-permute-start.21 = (f32[1,1,48,384]{3,2,1,0:T(8,128)S(1)}, f32[1,1,48,384]{3,2,1,0:T(8,128)S(1)}, u32[]{:S(2)}, u32[]{:S(2)}) collective-permute-start(f32[1,1,48,384]{3,2,1,0:T(8,128)S(1)} %get-tuple-element.157.refs_3_), channel_id=1, source_target_pairs={{0,2},{1,5},{2,0},{3,7},{4,6},{5,1},{6,4},{7,3},{8,10},{9,13},{10,... | collective-permute-start | bytes 221192 | tf_op jit(solution)/shard_map/ppermute | solution.py:640
  133.4 13.9 %collective-permute-start.19 = (f32[8,3,48,128]{3,2,1,0:T(8,128)S(1)}, f32[8,3,48,128]{3,2,1,0:T(8,128)S(1)}, u32[]{:S(2)}, u32[]{:S(2)}) collective-permute-start(f32[8,3,48,128]{3,2,1,0:T(8,128)S(1)} %get-tuple-element.164), channel_id=1, source_target_pairs={{0,4},{1,3},{2,6},{3,1},{4,0},{5,7},{6,2},{7,5},{8,12},{9,11},{10,... | collective-permute-start | bytes 1769480 | tf_op jit(solution)/shard_map/ppermute | solution.py:640
  134.6 18.1 %collective-permute-start.17 = (f32[2,3,48,384]{3,2,1,0:T(8,128)S(1)}, f32[2,3,48,384]{3,2,1,0:T(8,128)S(1)}, u32[]{:S(2)}, u32[]{:S(2)}) collective-permute-start(f32[2,3,48,384]{3,2,1,0:T(8,128)S(1)} %get-tuple-element.160.refs_3_), channel_id=1, source_target_pairs={{0,8},{1,9},{2,10},{3,11},{4,12},{5,13},{6,14},{7,15},{8,0},{9,1},... | collective-permute-start | bytes 1327112 | tf_op jit(solution)/shard_map/ppermute | solution.py:640
  136.5 10.8 %collective-permute-start.20 = (f32[3,16,48,128]{3,2,1,0:T(8,128)S(1)}, f32[3,16,48,128]{3,2,1,0:T(8,128)S(1)}, u32[]{:S(2)}, u32[]{:S(2)}) collective-permute-start(f32[3,16,48,128]{3,2,1,0:T(8,128)S(1)} %bitcast.33), channel_id=1, source_target_pairs={{0,1},{1,0},{2,3},{3,2},{4,5},{5,4},{6,7},{7,6},{8,9},{9,8},{10,11... | collective-permute-start | bytes 3538952 | tf_op jit(solution)/shard_map/ppermute | solution.py:640
  137.2 24.4 %collective-permute-start.26 = (f32[2,3,48,384]{3,2,1,0:T(8,128)S(1)}, f32[2,3,48,384]{3,2,1,0:T(8,128)S(1)}, u32[]{:S(2)}, u32[]{:S(2)}) collective-permute-start(f32[2,3,48,384]{3,2,1,0:T(8,128)S(1)} %get-tuple-element.172.refs_9_), channel_id=1, source_target_pairs={{0,16},{1,17},{2,18},{3,19},{4,20},{5,21},{6,22},{7,23},{8,24},{9,... | collective-permute-start | bytes 1327112 | tf_op jit(solution)/shard_map/ppermute | solution.py:640
  137.2 22.4 %collective-permute-start.15 = (f32[8,6,48,128]{3,2,1,0:T(8,128)S(1)}, f32[8,6,48,128]{3,2,1,0:T(8,128)S(1)}, u32[]{:S(2)}, u32[]{:S(2)}) collective-permute-start(f32[8,6,48,128]{3,2,1,0:T(8,128)S(1)} %get-tuple-element.155), channel_id=1, source_target_pairs={{0,4},{1,3},{2,6},{3,1},{4,0},{5,7},{6,2},{7,5},{8,12},{9,11},{10,... | collective-permute-start | bytes 3538952 | tf_op jit(solution)/shard_map/ppermute | solution.py:640
  148.1 9.4 %collective-permute-start.23 = (f32[2,1,48,384]{3,2,1,0:T(8,128)S(1)}, f32[2,1,48,384]{3,2,1,0:T(8,128)S(1)}, u32[]{:S(2)}, u32[]{:S(2)}) collective-permute-start(f32[2,1,48,384]{3,2,1,0:T(8,128)S(1)} %get-tuple-element.175.refs_3_), channel_id=1, source_target_pairs={{0,4},{1,3},{2,6},{3,1},{4,0},{5,7},{6,2},{7,5},{8,12},{9,11},{10,... | collective-permute-start | bytes 442376 | tf_op jit(solution)/shard_map/ppermute | solution.py:640
  151.1 12.3 %collective-permute-start.29 = (f32[16,768]{1,0:T(8,128)S(1)}, f32[16,768]{1,0:T(8,128)S(1)}, u32[]{:S(2)}, u32[]{:S(2)}) collective-permute-start(f32[16,768]{1,0:T(8,128)S(1)} %tick_10.1.refs_5_.refs_7_), channel_id=1, source_target_pairs={{0,2},{1,3},{2,0},{3,1},{4,6},{5,7},{6,4},{7,5},{8,10},{9,11},{10,... | collective-permute-start | bytes 147464 | tf_op jit(solution)/shard_map/ppermute | solution.py:640
  152.6 21.3 %collective-permute-start.28 = (f32[4,3,48,128]{3,2,1,0:T(8,128)S(1)}, f32[4,3,48,128]{3,2,1,0:T(8,128)S(1)}, u32[]{:S(2)}, u32[]{:S(2)}) collective-permute-start(f32[4,3,48,128]{3,2,1,0:T(8,128)S(1)} %get-tuple-element.184), channel_id=1, source_target_pairs={{0,8},{1,9},{2,10},{3,11},{4,12},{5,13},{6,14},{7,15},{8,0},{9,1},... | collective-permute-start | bytes 884744 | tf_op jit(solution)/shard_map/ppermute | solution.py:640
  157.5 25.2 %collective-permute-start.38 = (f32[8,3,48,128]{3,2,1,0:T(8,128)S(1)}, f32[8,3,48,128]{3,2,1,0:T(8,128)S(1)}, u32[]{:S(2)}, u32[]{:S(2)}) collective-permute-start(f32[8,3,48,128]{3,2,1,0:T(8,128)S(1)} %get-tuple-element.196), channel_id=1, source_target_pairs={{0,2},{1,5},{2,0},{3,7},{4,6},{5,1},{6,4},{7,3},{8,10},{9,13},{10,... | collective-permute-start | bytes 1769480 | tf_op jit(solution)/shard_map/ppermute | solution.py:640
  159.6 17.0 %collective-permute-start.31 = (f32[1,3,48,384]{3,2,1,0:T(8,128)S(1)}, f32[1,3,48,384]{3,2,1,0:T(8,128)S(1)}, u32[]{:S(2)}, u32[]{:S(2)}) collective-permute-start(f32[1,3,48,384]{3,2,1,0:T(8,128)S(1)} %get-tuple-element.177.refs_3_), channel_id=1, source_target_pairs={{0,16},{1,17},{2,18},{3,19},{4,20},{5,21},{6,22},{7,23},{8,24},{9,... | collective-permute-start | bytes 663560 | tf_op jit(solution)/shard_map/ppermute | solution.py:640
  161.5 12.4 %collective-permute-start.27 = (f32[1,1,48,384]{3,2,1,0:T(8,128)S(1)}, f32[1,1,48,384]{3,2,1,0:T(8,128)S(1)}, u32[]{:S(2)}, u32[]{:S(2)}) collective-permute-start(f32[1,1,48,384]{3,2,1,0:T(8,128)S(1)} %get-tuple-element.182), channel_id=1, source_target_pairs={{0,16},{1,17},{2,18},{3,19},{4,20},{5,21},{6,22},{7,23},{8,24},{9,... | collective-permute-start | bytes 221192 | tf_op jit(solution)/shard_map/ppermute | solution.py:640
  163.4 14.6 %collective-permute-start.32 = (f32[4,6,48,128]{3,2,1,0:T(8,128)S(1)}, f32[4,6,48,128]{3,2,1,0:T(8,128)S(1)}, u32[]{:S(2)}, u32[]{:S(2)}) collective-permute-start(f32[4,6,48,128]{3,2,1,0:T(8,128)S(1)} %get-tuple-element.178.refs_4_), channel_id=1, source_target_pairs={{0,2},{1,5},{2,0},{3,7},{4,6},{5,1},{6,4},{7,3},{8,10},{9,13},{10,... | collective-permute-start | bytes 1769480 | tf_op jit(solution)/shard_map/ppermute | solution.py:640
  174.5 7.6 %collective-permute-start.34 = (f32[1,3,48,384]{3,2,1,0:T(8,128)S(1)}, f32[1,3,48,384]{3,2,1,0:T(8,128)S(1)}, u32[]{:S(2)}, u32[]{:S(2)}) collective-permute-start(f32[1,3,48,384]{3,2,1,0:T(8,128)S(1)} %get-tuple-element.188.refs_5_), channel_id=1, source_target_pairs={{0,2},{1,5},{2,0},{3,7},{4,6},{5,1},{6,4},{7,3},{8,10},{9,13},{10,... | collective-permute-start | bytes 663560 | tf_op jit(solution)/shard_map/ppermute | solution.py:640
  176.0 6.1 %collective-permute-start.35 = (f32[2,3,48,128]{3,2,1,0:T(8,128)S(1)}, f32[2,3,48,128]{3,2,1,0:T(8,128)S(1)}, u32[]{:S(2)}, u32[]{:S(2)}) collective-permute-start(f32[2,3,48,128]{3,2,1,0:T(8,128)S(1)} %get-tuple-element.192), channel_id=1, source_target_pairs={{0,2},{1,5},{2,0},{3,7},{4,6},{5,1},{6,4},{7,3},{8,10},{9,13},{10,... | collective-permute-start | bytes 442376 | tf_op jit(solution)/shard_map/ppermute | solution.py:640
  176.6 4.1 %collective-permute-start.36 = (f32[16,768]{1,0:T(8,128)S(1)}, f32[16,768]{1,0:T(8,128)S(1)}, u32[]{:S(2)}, u32[]{:S(2)}) collective-permute-start(f32[16,768]{1,0:T(8,128)S(1)} %get-tuple-element.193.refs_5_), channel_id=1, source_target_pairs={{0,4},{1,5},{2,6},{3,7},{4,0},{5,1},{6,2},{7,3},{8,12},{9,13},{10,... | collective-permute-start | bytes 147464 | tf_op jit(solution)/shard_map/ppermute | solution.py:640
  178.7 11.4 %collective-permute-start.41 = (f32[2,6,48,128]{3,2,1,0:T(8,128)S(1)}, f32[2,6,48,128]{3,2,1,0:T(8,128)S(1)}, u32[]{:S(2)}, u32[]{:S(2)}) collective-permute-start(f32[2,6,48,128]{3,2,1,0:T(8,128)S(1)} %get-tuple-element.202), channel_id=1, source_target_pairs={{0,8},{1,9},{2,10},{3,11},{4,12},{5,13},{6,14},{7,15},{8,0},{9,1},... | collective-permute-start | bytes 884744 | tf_op jit(solution)/shard_map/ppermute | solution.py:640
  183.4 6.8 %collective-permute-start.39 = (f32[4,3,48,128]{3,2,1,0:T(8,128)S(1)}, f32[4,3,48,128]{3,2,1,0:T(8,128)S(1)}, u32[]{:S(2)}, u32[]{:S(2)}) collective-permute-start(f32[4,3,48,128]{3,2,1,0:T(8,128)S(1)} %get-tuple-element.198.refs_9_), channel_id=1, source_target_pairs={{0,4},{1,3},{2,6},{3,1},{4,0},{5,7},{6,2},{7,5},{8,12},{9,11},{10,... | collective-permute-start | bytes 884744 | tf_op jit(solution)/shard_map/ppermute | solution.py:640
  184.8 5.3 %collective-permute-start.40 = (f32[1,3,48,128]{3,2,1,0:T(8,128)S(1)}, f32[1,3,48,128]{3,2,1,0:T(8,128)S(1)}, u32[]{:S(2)}, u32[]{:S(2)}) collective-permute-start(f32[1,3,48,128]{3,2,1,0:T(8,128)S(1)} %get-tuple-element.200), channel_id=1, source_target_pairs={{0,16},{1,17},{2,18},{3,19},{4,20},{5,21},{6,22},{7,23},{8,24},{9,... | collective-permute-start | bytes 221192 | tf_op jit(solution)/shard_map/ppermute | solution.py:640
  184.8 4.1 %collective-permute-start.42 = (f32[16,768]{1,0:T(8,128)S(1)}, f32[16,768]{1,0:T(8,128)S(1)}, u32[]{:S(2)}, u32[]{:S(2)}) collective-permute-start(f32[16,768]{1,0:T(8,128)S(1)} %get-tuple-element.203.refs_7_), channel_id=1, source_target_pairs={{0,8},{1,9},{2,10},{3,11},{4,12},{5,13},{6,14},{7,15},{8,0},{9,1},... | collective-permute-start | bytes 147464 | tf_op jit(solution)/shard_map/ppermute | solution.py:640
  190.8 6.9 %collective-permute-start.45 = (f32[2,3,48,128]{3,2,1,0:T(8,128)S(1)}, f32[2,3,48,128]{3,2,1,0:T(8,128)S(1)}, u32[]{:S(2)}, u32[]{:S(2)}) collective-permute-start(f32[2,3,48,128]{3,2,1,0:T(8,128)S(1)} %get-tuple-element.208.refs_5_), channel_id=1, source_target_pairs={{0,8},{1,9},{2,10},{3,11},{4,12},{5,13},{6,14},{7,15},{8,0},{9,1},... | collective-permute-start | bytes 442376 | tf_op jit(solution)/shard_map/ppermute | solution.py:640
  190.8 6.8 %collective-permute-start.46 = (f32[16,768]{1,0:T(8,128)S(1)}, f32[16,768]{1,0:T(8,128)S(1)}, u32[]{:S(2)}, u32[]{:S(2)}) collective-permute-start(f32[16,768]{1,0:T(8,128)S(1)} %get-tuple-element.209.refs_3_), channel_id=1, source_target_pairs={{0,16},{1,17},{2,18},{3,19},{4,20},{5,21},{6,22},{7,23},{8,24},{9,... | collective-permute-start | bytes 147464 | tf_op jit(solution)/shard_map/ppermute | solution.py:640
  193.1 10.3 %collective-permute-start.44 = (f32[1,6,48,128]{3,2,1,0:T(8,128)S(1)}, f32[1,6,48,128]{3,2,1,0:T(8,128)S(1)}, u32[]{:S(2)}, u32[]{:S(2)}) collective-permute-start(f32[1,6,48,128]{3,2,1,0:T(8,128)S(1)} %get-tuple-element.206), channel_id=1, source_target_pairs={{0,16},{1,17},{2,18},{3,19},{4,20},{5,21},{6,22},{7,23},{8,24},{9,... | collective-permute-start | bytes 442376 | tf_op jit(solution)/shard_map/ppermute | solution.py:640
  198.2 6.0 %collective-permute-start.47 = (f32[1,3,48,128]{3,2,1,0:T(8,128)S(1)}, f32[1,3,48,128]{3,2,1,0:T(8,128)S(1)}, u32[]{:S(2)}, u32[]{:S(2)}) collective-permute-start(f32[1,3,48,128]{3,2,1,0:T(8,128)S(1)} %get-tuple-element.211.refs_5_), channel_id=1, source_target_pairs={{0,16},{1,17},{2,18},{3,19},{4,20},{5,21},{6,22},{7,23},{8,24},{9,... | collective-permute-start | bytes 221192 | tf_op jit(solution)/shard_map/ppermute | solution.py:640
  199.8 5.0 %collective-permute-start.25 = (f32[1,1,48,384]{3,2,1,0:T(8,128)S(1)}, f32[1,1,48,384]{3,2,1,0:T(8,128)S(1)}, u32[]{:S(2)}, u32[]{:S(2)}) collective-permute-start(f32[1,1,48,384]{3,2,1,0:T(8,128)S(1)} %get-tuple-element.179.refs_1_), channel_id=1, source_target_pairs={{0,1},{1,0},{2,3},{3,2},{4,5},{5,4},{6,7},{7,6},{8,9},{9,8},{10,11... | collective-permute-start | bytes 221192 | tf_op jit(solution)/shard_map/ppermute | solution.py:640
  199.8 5.5 %collective-permute-start.30 = (f32[1,1,48,384]{3,2,1,0:T(8,128)S(1)}, f32[1,1,48,384]{3,2,1,0:T(8,128)S(1)}, u32[]{:S(2)}, u32[]{:S(2)}) collective-permute-start(f32[1,1,48,384]{3,2,1,0:T(8,128)S(1)} %get-tuple-element.185.refs_3_), channel_id=1, source_target_pairs={{0,1},{1,0},{2,3},{3,2},{4,5},{5,4},{6,7},{7,6},{8,9},{9,8},{10,11... | collective-permute-start | bytes 221192 | tf_op jit(solution)/shard_map/ppermute | solution.py:640
  200.3 5.1 %collective-permute-start.37 = (f32[1,3,48,384]{3,2,1,0:T(8,128)S(1)}, f32[1,3,48,384]{3,2,1,0:T(8,128)S(1)}, u32[]{:S(2)}, u32[]{:S(2)}) collective-permute-start(f32[1,3,48,384]{3,2,1,0:T(8,128)S(1)} %get-tuple-element.194.refs_3_.refs_7_), channel_id=1, source_target_pairs={{0,1},{1,0},{2,3},{3,2},{4,5},{5,4},{6,7},{7,6},{8,9},{9,8},{10,11... | collective-permute-start | bytes 663560 | tf_op jit(solution)/shard_map/ppermute | solution.py:640
  203.4 2.0 collective-permute-start.33
  204.8 1.9 collective-permute-start.48
  204.8 1.5 collective-permute-start.43
  (20 other events, 158.6 us)

commit v2 on v1

--- a/solution.py
+++ b/solution.py
@@ -31,33 +31,7 @@
  'U': [(3, ((0, 1, 2, 3), (1, 0, 2, 3))), (1, ((2, 0, 1, 3), (2, 1, 0, 3)))],
  'F': [(3, ((1, 2, 0, 3), (0, 2, 1, 3))), (6, ((1, 0, 2, 3), (0, 1, 2, 3)))],
  'L': [(3, ((0, 1, 2, 3), (1, 0, 2, 3)))]}
-SCHEDULE = ['hidden',
- ('D0', 'D1'),
- 'middle',
- ('U0', 'U1', 'D1'),
- 'attend first',
- 'first heads',
- ('D0',),
- ('D1',),
- ('U0',),
- 'attend last',
- ('D1', 'U1', 'F0', 'F1'),
- 'last heads',
- ('U0',),
- ('D0',),
- 'input',
- ('U1', 'F0', 'L0', 'D1'),
- ('V',),
- ('U0', 'U1'),
- ('F1',),
- 'mix',
- ('D0', 'U1', 'F0', 'V'),
- ('U0', 'F1'),
- ('D0', 'F0', 'V'),
- ('L0',),
- ('L0', 'V', 'F0', 'F1'),
- ('V', 'L0'),
- ('F1', 'L0')]
+SCHEDULE = ['hidden', ('D0', 'D1'), 'middle', ('U0', 'U1', 'D1'), 'attend first', 'first heads', ('D0',), ('D1',), ('U0',), 'attend last', ('D1', 'U1', 'F0', 'F1'), 'last heads', ('U0',), ('D0',), 'input', ('U1', 'F0', 'L0', 'D1'), ('U0', 'U1', 'V'), ('F1',), 'mix', ('D0', 'U1', 'F0', 'V'), ('U0', 'F1'), ('D0', 'F0', 'V'), ('L0',), ('L0', 'F0', 'F1'), ('L0',), ('F1', 'L0')]
 COST = {'first_heads_grad': 0,
  'last_heads_grad': 0,
  'attend_back_first': 20,
@@ -710,12 +684,14 @@
 class Vectors:
     def __init__(self, total, n_dp):
         self.n_dp, self.total = n_dp, total
-        self.masks = [0] + [1 << b for b in range(n_dp.bit_length() - 1)]
+        self.rounds = [(0,)]
+        for bit in range(0, n_dp.bit_length() - 1, 2):
+            mask = 1 << bit
+            self.rounds.append((mask,) if 2 * mask >= n_dp else (mask, 2 * mask, 3 * mask))
         self.swap()
 
     def swap(self):
-        mask = self.masks.pop(0)
-        self.received = swap_with(self.total, self.n_dp, (mask, mask))
+        self.received = [swap_with(self.total, self.n_dp, (mask, mask)) for mask in self.rounds.pop(0)]
 
 
 def tick(pos, task, name, streams, after=(), vectors=None):
@@ -733,7 +709,7 @@
         jobs.append((stream, pairs, len(outs)))
         outs += [pltpu.VMEM(stream.dims, F32)] * (1 if stream.last else 2)
     if vectors is not None:
-        pair = (operand(vectors.total), operand(vectors.received))
+        parts = [operand(v) for v in [vectors.total] + vectors.received]
         outs.append(pltpu.VMEM((VECTORS, D), F32))
 
     scalars = [pos] + (list(task) if any(stream.weighted for stream in streams) else [])
@@ -763,7 +739,7 @@
                 else:
                     pl.loop(0, stream.dims[0])(act)
         if vectors is not None:
-            out_refs[-1][...] = ins[pair[0]][...] + ins[pair[1]][...]
+            out_refs[-1][...] = sum((ins[n][...] for n in parts[1:]), ins[parts[0]][...])
 
     return small_call(kernel, name, scalars, arrays, outs, after)
 
@@ -825,7 +801,7 @@
             n += 2
         if vectors is not None:
             vectors.total = sent[-1]
-            if vectors.masks:
+            if vectors.rounds:
                 vectors.swap()
             else:
                 vectors.received = None

time: 209 us -> 217 us (1.038)
  starting transfers between devices: 48.1 us -> 53.1 us
  waiting for transfers between devices: 24.4 us -> 26.6 us
    ppermute x50 -> x52, starting transfers between devices: 48.1 us -> 53.1 us  [swap_with(): return lax.ppermute(x, AXES, pairs)]
    ppermute x50 -> x52, waiting for transfers between devices: 24.4 us -> 26.6 us  [swap_with(): return lax.ppermute(x, AXES, pairs)]
    unnamed x36 -> x34, local copies, waits for them, and re-layouts: 3.84 us -> 4.74 us
    pallas_call x20 -> x19, Pallas kernels: 18.9 us -> 19.3 us  [small_call(): pl.pallas_call(body, in_specs=[SMEM] * len(scalars) + [vmem] * len(arrays...]
  transfers between devices with their start and end apart: 50 -> 52, of which waited for: 16 -> 13; matrix products, arithmetic and copies ran while one was open for 0% -> 0% of each run, Pallas kernels for 61% -> 59%
where the time goes in v2:
time: 217 us
  Pallas kernels  131 us (60%)
  starting transfers between devices  53.1 us (24%)
  waiting for transfers between devices  26.6 us (12%)
  local copies, waits for them, and re-layouts  4.74 us (2%)
    pallas_call x10, Pallas kernels, apply(): out = run(*args)  112 us
    ppermute x52, starting transfers between devices, swap_with(): return lax.ppermute(x, AXES, pairs)  53.1 us
    ppermute x52, waiting for transfers between devices, swap_with(): return lax.ppermute(x, AXES, pairs)  26.6 us
    pallas_call x19, Pallas kernels, small_call(): pl.pallas_call(body, in_specs=[SMEM] * len(scalars) + [vmem] * len(arrays...  19.3 us
    unnamed x34, local copies, waits for them, and re-layouts  4.74 us
  transfers between devices with their start and end apart: 52, of which 13 were waited for; matrix products, arithmetic and copies ran while one was open for 0% of the time, Pallas kernels for 59%

profile of v2, /device:TPU:0, one launch (start us, length us, event | category | flops | bytes accessed | tf_op | source)
XLA Modules:
  0.0 217.2 jit_solution(14535089315159562786)
XLA Ops:
  1.3 4.0 %collective-permute-start.2 = (s32[3]{0:T(128)S(1)}, s32[3]{0:T(128)S(1)}, u32[]{:S(2)}, u32[]{:S(2)}) collective-permute-start(s32[3]{0:T(128)S(1)} %compare_select_fusion), channel_id=1, source_target_pairs={{0,6},{1,7},{2,4},{3,5},{4,2},{5,3},{6,0},{7,1},{8,14},{9,15},{10,... | collective-permute-start | bytes 44 | tf_op jit(solution)/shard_map/ppermute | solution.py:614
  6.0 22.1 %forward.1 = (bf16[3,1024,768]{2,1,0:T(8,128)(2,1)}, bf16[1024,768]{1,0:T(8,128)(2,1)}, bf16[1024,768]{1,0:T(8,128)(2,1)}, bf16[6,8,384,256]{3,2,1,0:T(8,128)(2,...) custom-call(bf16[1024,768]{1,0:T(8,128)(2,1)} %bitcast.31, s32[1,1024]{1,0:T(1,128)} %seg_ref.1, f32[768]{0:T(1024)} %refs_2_.5, ...), custom_call_target="tpu_custom_call" | custom-call | flops 96000000000 | bytes 24 | tf_op jit(solution)/shard_map/forward/pallas_call | solution.py:94
  28.1 4.1 %collective-permute-start.5 = (s32[3]{0:T(128)S(1)}, s32[3]{0:T(128)S(1)}, u32[]{:S(2)}, u32[]{:S(2)}) collective-permute-start(s32[3]{0:T(128)S(1)} %add_add_fusion.1.refs_5_), channel_id=1, source_target_pairs={{0,24},{1,25},{2,26},{3,27},{4,28},{5,29},{6,30},{7,31},{8,16},{9,... | collective-permute-start | bytes 44 | tf_op jit(solution)/shard_map/ppermute | solution.py:614
  32.9 16.7 %up_and_down_grad.1 = (bf16[1024,3072]{1,0:T(8,128)(2,1)}, bf16[1024,3072]{1,0:T(8,128)(2,1)}, f32[3072,384]{1,0:T(8,128)S(1)}, f32[3072,384]{1,0:T(8,128)}) custom-call(s32[2]{0:T(128)S(1)} %pad_add_fusion.refs_0_.pos_ref, bf16[1024,768]{1,0:T(8,128)(2,1)} %get-tuple-element.122.refs_1_.in_ref, bf16[1024,768]{1,0:T(8,128)(2,1)} %bitcast.29, ...), custom_call_target="tpu_custom_call" | custom-call | flops 64000000000 | bytes 16 | tf_op jit(solution)/shard_map/up_and_down_grad/pallas_call | solution.py:94
  49.7 16.6 %hidden_grad.1 = (bf16[1024,3072]{1,0:T(8,128)(2,1)S(1)}, bf16[1024,768]{1,0:T(8,128)(2,1)S(1)}, f32[4,768,384]{2,1,0:T(8,128)}, f32[4,768,384]{2,1,0:T(8,128)}, f32[4,1,768]{2,1,0:T(1,128)}, /*index=5*/f32[1,768]{1,0:T(1,128)}) custom-call(s32[2]{0:T(128)S(1)} %pad_add_fusion.refs_0_.pos_ref, s32[3]{0:T(128)S(1)} %add_add_fusion.counts_ref.refs_1_, ...), custom_call_target="tpu_custom_call" | custom-call | flops 240000008192 | bytes 14 | tf_op jit(solution)/shard_map/hidden_grad/pallas_call | solution.py:94
  66.3 2.6 %copy-done.1 = bf16[1024,3072]{1,0:T(8,128)(2,1)} copy-done((bf16[1024,3072]{1,0:T(8,128)(2,1)}, bf16[1024,3072]{1,0:T(8,128)(2,1)S(1)}, u32[]{:S(2)}) %copy-start.1) | copy-done | bytes 6291480
  69.4 3.2 %tick_1.1 = (f32[8,3,48,384]{3,2,1,0:T(8,128)S(1)}, f32[8,3,48,384]{3,2,1,0:T(8,128)S(1)}, f32[8,1,48,384]{3,2,1,0:T(8,128)S(1)}, f32[8,1,48,384]{3,2,1,0:T(8,128)S(1)}) custom-call(s32[2]{0:T(128)S(1)} %pad_add_fusion.refs_0_.pos_ref, s32[3]{0:T(128)S(1)} %add_add_fusion.counts_ref.refs_1_, s32[1]{0:T(128)} %copy.33.label_ref.refs_2_, ...), custom_call_target="tpu_custom_call" | custom-call | flops 1000000000 | bytes 1 | tf_op jit(solution)/shard_map/tick_1/pallas_call | solution.py:628
  72.6 1.4 collective-permute-start.8
  74.0 1.5 collective-permute-start.10
  75.6 12.2 %norm_two_back.1 = (f32[1024,768]{1,0:T(8,128)}, bf16[1024,768]{1,0:T(8,128)(2,1)}, bf16[1024,768]{1,0:T(8,128)(2,1)}, f32[3,768]{1,0:T(4,128)}) custom-call(bf16[1024,768]{1,0:T(8,128)(2,1)S(1)} %get-tuple-element.132.refs_0_, f32[1024,768]{1,0:T(8,128)} %get-tuple-element.121.refs_1_.refs_0_, f32[768]{0:T(1024)} %refs_2_.4, ...), custom_call_target="tpu_custom_call" | custom-call | flops 12000000000 | bytes 16 | tf_op jit(solution)/shard_map/norm_two_back/pallas_call | solution.py:94
  87.9 2.0 tick_2.1
  89.9 2.9 %collective-permute-start.9 = (f32[4,1,48,384]{3,2,1,0:T(8,128)S(1)}, f32[4,1,48,384]{3,2,1,0:T(8,128)S(1)}, u32[]{:S(2)}, u32[]{:S(2)}) collective-permute-start(f32[4,1,48,384]{3,2,1,0:T(8,128)S(1)} %get-tuple-element.136), channel_id=1, source_target_pairs={{0,16},{1,17},{2,18},{3,19},{4,20},{5,21},{6,22},{7,23},{8,24},{9,... | collective-permute-start | bytes 884744 | tf_op jit(solution)/shard_map/ppermute | solution.py:614
  92.8 1.4 collective-permute-start.12
  94.2 1.5 collective-permute-start.14
  95.7 9.5 %attend_back_first.1.refs_2_.refs_5_.refs_3_ = bf16[3,1024,512]{2,1,0:T(8,128)(2,1)S(1)} custom-call(bf16[3,1024,768]{2,1,0:T(8,128)(2,1)} %get-tuple-element.139.refs_0_.refs_1_.refs_2_, bf16[3,1024,768]{2,1,0:T(8,128)(2,1)} %get-tuple-element.139.refs_0_.refs_1_.refs_2_, bf16[3,1024,768]{2,1,0:T(8,128)(2,1)} %get-tuple-element.139.refs_0_.refs_1_.refs_2_, ...), custom_call_target="tpu_custom_call" | custom-call | flops 80000000000 | bytes 12 | tf_op jit(solution)/shard_map/attend_back_first/pallas_call | solution.py:94
  105.3 7.9 %first_heads_grad.1 = (f32[9,768,128]{2,1,0:T(8,128)}, f32[9,768,128]{2,1,0:T(8,128)}) custom-call(s32[2]{0:T(128)S(1)} %pad_add_fusion.refs_0_.pos_ref, bf16[1024,768]{1,0:T(8,128)(2,1)S(1)} %copy-done.5, bf16[3,1024,512]{2,1,0:T(8,128)(2,1)S(1)} %attend_back_first.1.refs_2_.refs_5_.refs_3_, bf16[1024,768]{1,0:T(8,128)(2,1)} %get-tuple-element.142.refs_3_, ...), custom_call_target="tpu_custom_call" | custom-call | bytes 10 | tf_op jit(solution)/shard_map/first_heads_grad/pallas_call | solution.py:94
  113.2 1.6 tick_3.1
  116.0 1.3 collective-permute-start.11
  120.0 6.0 %attend_back_last.1.refs_7_.refs_2_.refs_4_ = bf16[3,1024,256]{2,1,0:T(8,128)(2,1)S(1)} custom-call(bf16[3,1024,768]{2,1,0:T(8,128)(2,1)} %get-tuple-element.139.refs_0_.refs_1_.refs_2_, bf16[3,1024,768]{2,1,0:T(8,128)(2,1)} %get-tuple-element.139.refs_0_.refs_1_.refs_2_, bf16[3,1024,768]{2,1,0:T(8,128)(2,1)} %get-tuple-element.139.refs_0_.refs_1_.refs_2_, ...), custom_call_target="tpu_custom_call" | custom-call | flops 80000000000 | bytes 6 | tf_op jit(solution)/shard_map/attend_back_last/pallas_call | solution.py:94
  125.9 1.1 copy-done.3
  127.1 1.7 tick_6.1
  128.8 1.6 collective-permute-start.18
  130.9 3.4 %last_heads_grad.1 = (f32[3,768,128]{2,1,0:T(8,128)}, f32[3,768,128]{2,1,0:T(8,128)}) custom-call(s32[2]{0:T(128)S(1)} %pad_add_fusion.refs_0_.pos_ref, bf16[1024,768]{1,0:T(8,128)(2,1)S(1)} %copy-done.5, bf16[3,1024,256]{2,1,0:T(8,128)(2,1)S(1)} %copy-done.4, f32[1,1,48,384]{3,2,1,0:T(8,128)S(1)} %get-tuple-element.156.refs_3_), custom_call_target="tpu_custom_call" | custom-call | bytes 5 | tf_op jit(solution)/shard_map/last_heads_grad/pallas_call | solution.py:94
  134.3 1.1 collective-permute-start.19
  136.0 1.8 collective-permute-start.17
  138.6 1.3 collective-permute-start.15
  139.9 8.5 %norm_one_back.1 = (bf16[1024,768]{1,0:T(8,128)(2,1)}, f32[16,768]{1,0:T(8,128)}) custom-call(bf16[1024,768]{1,0:T(8,128)(2,1)} %bitcast.32, f32[1024,768]{1,0:T(8,128)} %get-tuple-element.166.refs_1_, f32[768]{0:T(1024)} %refs_2_.5, bf16[3,1024,512]{2,1,0:T(8,128)(2,1)S(1)} %attend_back_first.1.refs_2_.refs_5_.refs_3_, bf16[3,1024,256]{2,1,0:T(8,128)(2,1)S(1)} %copy-done.4, ...), custom_call_target="tpu_custom_call" | custom-call | flops 12000000000 | bytes 10 | tf_op jit(solution)/shard_map/norm_one_back/pallas_call | solution.py:94
  150.1 1.2 collective-permute-done.24.refs_6_
  152.0 6.4 %collective-permute-done.23.refs_4_ = f32[2,1,48,384]{3,2,1,0:T(8,128)S(1)} collective-permute-done((f32[2,1,48,384]{3,2,1,0:T(8,128)S(1)}, f32[2,1,48,384]{3,2,1,0:T(8,128)S(1)}, u32[]{:S(2)}, u32[]{:S(2)}) %collective-permute-start.23) | collective-permute-done | bytes 147488 | tf_op jit(solution)/shard_map/ppermute | solution.py:614
  159.0 1.5 collective-permute-start.31
  160.5 1.5 collective-permute-start.30
  163.3 1.6 collective-permute-start.42
  165.3 2.5 %collective-permute-start.27 = (f32[1,1,48,384]{3,2,1,0:T(8,128)S(1)}, f32[1,1,48,384]{3,2,1,0:T(8,128)S(1)}, u32[]{:S(2)}, u32[]{:S(2)}) collective-permute-start(f32[1,1,48,384]{3,2,1,0:T(8,128)S(1)} %get-tuple-element.181), channel_id=1, source_target_pairs={{0,16},{1,17},{2,18},{3,19},{4,20},{5,21},{6,22},{7,23},{8,24},{9,... | collective-permute-start | bytes 221192 | tf_op jit(solution)/shard_map/ppermute | solution.py:614
  168.6 8.7 %mix.1.refs_11_ = bf16[1024,768]{1,0:T(8,128)(2,1)} custom-call(f32[1024,768]{1,0:T(8,128)} %get-tuple-element.121.refs_1_.refs_0_, bf16[1024,3072]{1,0:T(8,128)(2,1)} %get-tuple-element.123.refs_1_, bf16[3072,768]{1,0:T(8,128)(2,1)S(1)} %bitcast.24, f32[768]{0:T(1024)} %refs_3_.3, f32[4,6,48,128]{3,2,1,0:T(8,128)S(1)} %get-tuple-element.177.refs_4_), custom_call_target="tpu_custom_call" | custom-call | flops 80000000000 | bytes 10 | tf_op jit(solution)/shard_map/mix/pallas_call | solution.py:94
  177.3 1.1 collective-permute-done.27.refs_4_
  179.0 1.0 collective-permute-start.36
  180.0 1.5 collective-permute-start.40
  181.5 4.4 %collective-permute-done.40.refs_8_ = f32[16,768]{1,0:T(8,128)S(1)} collective-permute-done((f32[16,768]{1,0:T(8,128)S(1)}, f32[16,768]{1,0:T(8,128)S(1)}, u32[]{:S(2)}, u32[]{:S(2)}) %collective-permute-start.40) | collective-permute-done | bytes 49184 | tf_op jit(solution)/shard_map/ppermute | solution.py:614
  185.9 1.1 collective-permute-start.37
  187.0 1.7 collective-permute-start.38
  189.4 2.8 %collective-permute-done.39.refs_7_ = f32[16,768]{1,0:T(8,128)S(1)} collective-permute-done((f32[16,768]{1,0:T(8,128)S(1)}, f32[16,768]{1,0:T(8,128)S(1)}, u32[]{:S(2)}, u32[]{:S(2)}) %collective-permute-start.39) | collective-permute-done | bytes 49184 | tf_op jit(solution)/shard_map/ppermute | solution.py:614
  194.3 2.5 %collective-permute-start.44 = (f32[1,3,48,128]{3,2,1,0:T(8,128)S(1)}, f32[1,3,48,128]{3,2,1,0:T(8,128)S(1)}, u32[]{:S(2)}, u32[]{:S(2)}) collective-permute-start(f32[1,3,48,128]{3,2,1,0:T(8,128)S(1)} %get-tuple-element.200), channel_id=1, source_target_pairs={{0,16},{1,17},{2,18},{3,19},{4,20},{5,21},{6,22},{7,23},{8,24},{9,... | collective-permute-start | bytes 221192 | tf_op jit(solution)/shard_map/ppermute | solution.py:614
  196.8 2.9 %collective-permute-done.44.refs_4_ = f32[1,3,48,128]{3,2,1,0:T(8,128)S(1)} collective-permute-done((f32[1,3,48,128]{3,2,1,0:T(8,128)S(1)}, f32[1,3,48,128]{3,2,1,0:T(8,128)S(1)}, u32[]{:S(2)}, u32[]{:S(2)}) %collective-permute-start.44) | collective-permute-done | bytes 73760 | tf_op jit(solution)/shard_map/ppermute | solution.py:614
  200.8 2.2 %collective-permute-start.48 = (f32[2,3,48,128]{3,2,1,0:T(8,128)S(1)}, f32[2,3,48,128]{3,2,1,0:T(8,128)S(1)}, u32[]{:S(2)}, u32[]{:S(2)}) collective-permute-start(f32[2,3,48,128]{3,2,1,0:T(8,128)S(1)} %get-tuple-element.207.refs_3_), channel_id=1, source_target_pairs={{0,8},{1,9},{2,10},{3,11},{4,12},{5,13},{6,14},{7,15},{8,0},{9,1},... | collective-permute-start | bytes 442376 | tf_op jit(solution)/shard_map/ppermute | solution.py:614
  203.8 3.2 %collective-permute-done.48.refs_2_ = f32[2,3,48,128]{3,2,1,0:T(8,128)S(1)} collective-permute-done((f32[2,3,48,128]{3,2,1,0:T(8,128)S(1)}, f32[2,3,48,128]{3,2,1,0:T(8,128)S(1)}, u32[]{:S(2)}, u32[]{:S(2)}) %collective-permute-start.48) | collective-permute-done | bytes 147488 | tf_op jit(solution)/shard_map/ppermute | solution.py:614
  207.6 2.0 collective-permute-start.49
  210.7 2.3 %collective-permute-done.49.refs_4_ = f32[1,3,48,128]{3,2,1,0:T(8,128)S(1)} collective-permute-done((f32[1,3,48,128]{3,2,1,0:T(8,128)S(1)}, f32[1,3,48,128]{3,2,1,0:T(8,128)S(1)}, u32[]{:S(2)}, u32[]{:S(2)}) %collective-permute-start.49) | collective-permute-done | bytes 73760 | tf_op jit(solution)/shard_map/ppermute | solution.py:614
  215.4 1.8 place.1
  (125 shorter events, 22.5 us)
Async XLA Ops:
  1.3 26.8 %collective-permute-start.2 = (s32[3]{0:T(128)S(1)}, s32[3]{0:T(128)S(1)}, u32[]{:S(2)}, u32[]{:S(2)}) collective-permute-start(s32[3]{0:T(128)S(1)} %compare_select_fusion), channel_id=1, source_target_pairs={{0,6},{1,7},{2,4},{3,5},{4,2},{5,3},{6,0},{7,1},{8,14},{9,15},{10,... | collective-permute-start | bytes 44 | tf_op jit(solution)/shard_map/ppermute | solution.py:614
  5.3 22.9 %collective-permute-start.1 = (s32[3]{0:T(128)S(1)}, s32[3]{0:T(128)S(1)}, u32[]{:S(2)}, u32[]{:S(2)}) collective-permute-start(s32[3]{0:T(128)S(1)} %compare_select_fusion), channel_id=1, source_target_pairs={{0,4},{1,5},{2,6},{3,7},{4,0},{5,1},{6,2},{7,3},{8,12},{9,13},{10,... | collective-permute-start | bytes 44 | tf_op jit(solution)/shard_map/ppermute | solution.py:614
  5.8 22.4 %collective-permute-start = (s32[3]{0:T(128)S(1)}, s32[3]{0:T(128)S(1)}, u32[]{:S(2)}, u32[]{:S(2)}) collective-permute-start(s32[3]{0:T(128)S(1)} %compare_select_fusion), channel_id=1, source_target_pairs={{0,2},{1,3},{2,0},{3,1},{4,6},{5,7},{6,4},{7,5},{8,10},{9,11},{10,... | collective-permute-start | bytes 44 | tf_op jit(solution)/shard_map/ppermute | solution.py:614
  28.1 21.5 %collective-permute-start.5 = (s32[3]{0:T(128)S(1)}, s32[3]{0:T(128)S(1)}, u32[]{:S(2)}, u32[]{:S(2)}) collective-permute-start(s32[3]{0:T(128)S(1)} %add_add_fusion.1.refs_5_), channel_id=1, source_target_pairs={{0,24},{1,25},{2,26},{3,27},{4,28},{5,29},{6,30},{7,31},{8,16},{9,... | collective-permute-start | bytes 44 | tf_op jit(solution)/shard_map/ppermute | solution.py:614
  32.2 17.4 %collective-permute-start.4 = (s32[3]{0:T(128)S(1)}, s32[3]{0:T(128)S(1)}, u32[]{:S(2)}, u32[]{:S(2)}) collective-permute-start(s32[3]{0:T(128)S(1)} %add_add_fusion.1.refs_5_), channel_id=1, source_target_pairs={{0,16},{1,17},{2,18},{3,19},{4,20},{5,21},{6,22},{7,23},{8,24},{9,... | collective-permute-start | bytes 44 | tf_op jit(solution)/shard_map/ppermute | solution.py:614
  32.2 17.4 %collective-permute-start.3 = (s32[3]{0:T(128)S(1)}, s32[3]{0:T(128)S(1)}, u32[]{:S(2)}, u32[]{:S(2)}) collective-permute-start(s32[3]{0:T(128)S(1)} %add_add_fusion.1.refs_5_), channel_id=1, source_target_pairs={{0,8},{1,9},{2,10},{3,11},{4,12},{5,13},{6,14},{7,15},{8,0},{9,1},... | collective-permute-start | bytes 44 | tf_op jit(solution)/shard_map/ppermute | solution.py:614
  49.6 19.8 %collective-permute-start.7 = (f32[16,4,48,384]{3,2,1,0:T(8,128)}, f32[16,4,48,384]{3,2,1,0:T(8,128)}, u32[]{:S(2)}, u32[]{:S(2)}) collective-permute-start(f32[16,4,48,384]{3,2,1,0:T(8,128)} %bitcast.27), channel_id=1, source_target_pairs={{0,1},{1,0},{2,3},{3,2},{4,5},{5,4},{6,7},{7,6},{8,9},{9,8},{10,11... | collective-permute-start | bytes 14155784 | tf_op jit(solution)/shard_map/ppermute | solution.py:614
  68.9 18.9 %collective-permute-start.6 = (f32[4,16,48,384]{3,2,1,0:T(8,128)}, f32[4,16,48,384]{3,2,1,0:T(8,128)S(1)}, u32[]{:S(2)}, u32[]{:S(2)}) collective-permute-start(f32[4,16,48,384]{3,2,1,0:T(8,128)} %bitcast.26), channel_id=1, source_target_pairs={{0,1},{1,0},{2,3},{3,2},{4,5},{5,4},{6,7},{7,6},{8,9},{9,8},{10,11... | collective-permute-start | bytes 14155784 | tf_op jit(solution)/shard_map/ppermute | solution.py:614
  72.6 15.3 %collective-permute-start.8 = (f32[8,1,48,384]{3,2,1,0:T(8,128)S(1)}, f32[8,1,48,384]{3,2,1,0:T(8,128)S(1)}, u32[]{:S(2)}, u32[]{:S(2)}) collective-permute-start(f32[8,1,48,384]{3,2,1,0:T(8,128)S(1)} %get-tuple-element.131), channel_id=1, source_target_pairs={{0,8},{1,9},{2,10},{3,11},{4,12},{5,13},{6,14},{7,15},{8,0},{9,1},... | collective-permute-start | bytes 1769480 | tf_op jit(solution)/shard_map/ppermute | solution.py:614
  74.0 39.2 %collective-permute-start.10 = (f32[8,3,48,384]{3,2,1,0:T(8,128)S(1)}, f32[8,3,48,384]{3,2,1,0:T(8,128)S(1)}, u32[]{:S(2)}, u32[]{:S(2)}) collective-permute-start(f32[8,3,48,384]{3,2,1,0:T(8,128)S(1)} %get-tuple-element.133.refs_6_), channel_id=1, source_target_pairs={{0,4},{1,3},{2,6},{3,1},{4,0},{5,7},{6,2},{7,5},{8,12},{9,11},{10,... | collective-permute-start | bytes 5308424 | tf_op jit(solution)/shard_map/ppermute | solution.py:614
  89.9 25.5 %collective-permute-start.9 = (f32[4,1,48,384]{3,2,1,0:T(8,128)S(1)}, f32[4,1,48,384]{3,2,1,0:T(8,128)S(1)}, u32[]{:S(2)}, u32[]{:S(2)}) collective-permute-start(f32[4,1,48,384]{3,2,1,0:T(8,128)S(1)} %get-tuple-element.136), channel_id=1, source_target_pairs={{0,16},{1,17},{2,18},{3,19},{4,20},{5,21},{6,22},{7,23},{8,24},{9,... | collective-permute-start | bytes 884744 | tf_op jit(solution)/shard_map/ppermute | solution.py:614
  92.8 34.3 %collective-permute-start.12 = (f32[8,1,48,384]{3,2,1,0:T(8,128)}, f32[8,1,48,384]{3,2,1,0:T(8,128)}, u32[]{:S(2)}, u32[]{:S(2)}) collective-permute-start(f32[8,1,48,384]{3,2,1,0:T(8,128)} %get-tuple-element.149), channel_id=1, source_target_pairs={{0,8},{1,9},{2,10},{3,11},{4,12},{5,13},{6,14},{7,15},{8,0},{9,1},... | collective-permute-start | bytes 1769480 | tf_op jit(solution)/shard_map/ppermute | solution.py:614
  94.2 23.1 %collective-permute-start.14 = (f32[8,3,48,384]{3,2,1,0:T(8,128)S(1)}, f32[8,3,48,384]{3,2,1,0:T(8,128)S(1)}, u32[]{:S(2)}, u32[]{:S(2)}) collective-permute-start(f32[8,3,48,384]{3,2,1,0:T(8,128)S(1)} %get-tuple-element.141.refs_5_), channel_id=1, source_target_pairs={{0,2},{1,5},{2,0},{3,7},{4,6},{5,1},{6,4},{7,3},{8,10},{9,13},{10,... | collective-permute-start | bytes 5308424 | tf_op jit(solution)/shard_map/ppermute | solution.py:614
  113.2 13.9 %collective-permute-start.13 = (f32[9,16,48,128]{3,2,1,0:T(8,128)}, f32[9,16,48,128]{3,2,1,0:T(8,128)S(1)}, u32[]{:S(2)}, u32[]{:S(2)}) collective-permute-start(f32[9,16,48,128]{3,2,1,0:T(8,128)} %bitcast.28), channel_id=1, source_target_pairs={{0,1},{1,0},{2,3},{3,2},{4,5},{5,4},{6,7},{7,6},{8,9},{9,8},{10,11... | collective-permute-start | bytes 10616840 | tf_op jit(solution)/shard_map/ppermute | solution.py:614
  114.9 23.0 %collective-permute-start.22 = (f32[4,3,48,384]{3,2,1,0:T(8,128)}, f32[4,3,48,384]{3,2,1,0:T(8,128)S(1)}, u32[]{:S(2)}, u32[]{:S(2)}) collective-permute-start(f32[4,3,48,384]{3,2,1,0:T(8,128)} %get-tuple-element.145.refs_3_), channel_id=1, source_target_pairs={{0,8},{1,9},{2,10},{3,11},{4,12},{5,13},{6,14},{7,15},{8,0},{9,1},... | collective-permute-start | bytes 2654216 | tf_op jit(solution)/shard_map/ppermute | solution.py:614
  116.0 11.0 %collective-permute-start.11 = (f32[2,1,48,384]{3,2,1,0:T(8,128)S(1)}, f32[2,1,48,384]{3,2,1,0:T(8,128)S(1)}, u32[]{:S(2)}, u32[]{:S(2)}) collective-permute-start(f32[2,1,48,384]{3,2,1,0:T(8,128)S(1)} %get-tuple-element.147.refs_3_), channel_id=1, source_target_pairs={{0,4},{1,3},{2,6},{3,1},{4,0},{5,7},{6,2},{7,5},{8,12},{9,11},{10,... | collective-permute-start | bytes 442376 | tf_op jit(solution)/shard_map/ppermute | solution.py:614
  119.0 16.4 %collective-permute-start.16 = (f32[4,3,48,384]{3,2,1,0:T(8,128)S(1)}, f32[4,3,48,384]{3,2,1,0:T(8,128)S(1)}, u32[]{:S(2)}, u32[]{:S(2)}) collective-permute-start(f32[4,3,48,384]{3,2,1,0:T(8,128)S(1)} %get-tuple-element.152.refs_5_), channel_id=1, source_target_pairs={{0,4},{1,3},{2,6},{3,1},{4,0},{5,7},{6,2},{7,5},{8,12},{9,11},{10,... | collective-permute-start | bytes 2654216 | tf_op jit(solution)/shard_map/ppermute | solution.py:614
  128.8 9.8 %collective-permute-start.18 = (f32[4,1,48,384]{3,2,1,0:T(8,128)S(1)}, f32[4,1,48,384]{3,2,1,0:T(8,128)S(1)}, u32[]{:S(2)}, u32[]{:S(2)}) collective-permute-start(f32[4,1,48,384]{3,2,1,0:T(8,128)S(1)} %get-tuple-element.161), channel_id=1, source_target_pairs={{0,2},{1,5},{2,0},{3,7},{4,6},{5,1},{6,4},{7,3},{8,10},{9,13},{10,... | collective-permute-start | bytes 884744 | tf_op jit(solution)/shard_map/ppermute | solution.py:614
  130.4 8.1 %collective-permute-start.21 = (f32[1,1,48,384]{3,2,1,0:T(8,128)S(1)}, f32[1,1,48,384]{3,2,1,0:T(8,128)S(1)}, u32[]{:S(2)}, u32[]{:S(2)}) collective-permute-start(f32[1,1,48,384]{3,2,1,0:T(8,128)S(1)} %get-tuple-element.156.refs_3_), channel_id=1, source_target_pairs={{0,2},{1,5},{2,0},{3,7},{4,6},{5,1},{6,4},{7,3},{8,10},{9,13},{10,... | collective-permute-start | bytes 221192 | tf_op jit(solution)/shard_map/ppermute | solution.py:614
  134.3 14.1 %collective-permute-start.19 = (f32[8,3,48,128]{3,2,1,0:T(8,128)S(1)}, f32[8,3,48,128]{3,2,1,0:T(8,128)S(1)}, u32[]{:S(2)}, u32[]{:S(2)}) collective-permute-start(f32[8,3,48,128]{3,2,1,0:T(8,128)S(1)} %get-tuple-element.163), channel_id=1, source_target_pairs={{0,4},{1,3},{2,6},{3,1},{4,0},{5,7},{6,2},{7,5},{8,12},{9,11},{10,... | collective-permute-start | bytes 1769480 | tf_op jit(solution)/shard_map/ppermute | solution.py:614
  136.0 16.0 %collective-permute-start.17 = (f32[2,3,48,384]{3,2,1,0:T(8,128)S(1)}, f32[2,3,48,384]{3,2,1,0:T(8,128)S(1)}, u32[]{:S(2)}, u32[]{:S(2)}) collective-permute-start(f32[2,3,48,384]{3,2,1,0:T(8,128)S(1)} %get-tuple-element.159.refs_3_), channel_id=1, source_target_pairs={{0,8},{1,9},{2,10},{3,11},{4,12},{5,13},{6,14},{7,15},{8,0},{9,1},... | collective-permute-start | bytes 1327112 | tf_op jit(solution)/shard_map/ppermute | solution.py:614
  137.8 10.6 %collective-permute-start.20 = (f32[3,16,48,128]{3,2,1,0:T(8,128)}, f32[3,16,48,128]{3,2,1,0:T(8,128)S(1)}, u32[]{:S(2)}, u32[]{:S(2)}) collective-permute-start(f32[3,16,48,128]{3,2,1,0:T(8,128)} %bitcast.33), channel_id=1, source_target_pairs={{0,1},{1,0},{2,3},{3,2},{4,5},{5,4},{6,7},{7,6},{8,9},{9,8},{10,11... | collective-permute-start | bytes 3538952 | tf_op jit(solution)/shard_map/ppermute | solution.py:614
  138.5 24.8 %collective-permute-start.26 = (f32[2,3,48,384]{3,2,1,0:T(8,128)S(1)}, f32[2,3,48,384]{3,2,1,0:T(8,128)S(1)}, u32[]{:S(2)}, u32[]{:S(2)}) collective-permute-start(f32[2,3,48,384]{3,2,1,0:T(8,128)S(1)} %get-tuple-element.171.refs_9_), channel_id=1, source_target_pairs={{0,16},{1,17},{2,18},{3,19},{4,20},{5,21},{6,22},{7,23},{8,24},{9,... | collective-permute-start | bytes 1327112 | tf_op jit(solution)/shard_map/ppermute | solution.py:614
  138.6 23.5 %collective-permute-start.15 = (f32[8,6,48,128]{3,2,1,0:T(8,128)S(1)}, f32[8,6,48,128]{3,2,1,0:T(8,128)S(1)}, u32[]{:S(2)}, u32[]{:S(2)}) collective-permute-start(f32[8,6,48,128]{3,2,1,0:T(8,128)S(1)} %get-tuple-element.154), channel_id=1, source_target_pairs={{0,4},{1,3},{2,6},{3,1},{4,0},{5,7},{6,2},{7,5},{8,12},{9,11},{10,... | collective-permute-start | bytes 3538952 | tf_op jit(solution)/shard_map/ppermute | solution.py:614
  149.2 9.2 %collective-permute-start.23 = (f32[2,1,48,384]{3,2,1,0:T(8,128)S(1)}, f32[2,1,48,384]{3,2,1,0:T(8,128)S(1)}, u32[]{:S(2)}, u32[]{:S(2)}) collective-permute-start(f32[2,1,48,384]{3,2,1,0:T(8,128)S(1)} %get-tuple-element.174.refs_7_), channel_id=1, source_target_pairs={{0,4},{1,3},{2,6},{3,1},{4,0},{5,7},{6,2},{7,5},{8,12},{9,11},{10,... | collective-permute-start | bytes 442376 | tf_op jit(solution)/shard_map/ppermute | solution.py:614
  151.3 27.1 %collective-permute-start.28 = (f32[4,3,48,128]{3,2,1,0:T(8,128)S(1)}, f32[4,3,48,128]{3,2,1,0:T(8,128)S(1)}, u32[]{:S(2)}, u32[]{:S(2)}) collective-permute-start(f32[4,3,48,128]{3,2,1,0:T(8,128)S(1)} %get-tuple-element.183), channel_id=1, source_target_pairs={{0,8},{1,9},{2,10},{3,11},{4,12},{5,13},{6,14},{7,15},{8,0},{9,1},... | collective-permute-start | bytes 884744 | tf_op jit(solution)/shard_map/ppermute | solution.py:614
  159.0 5.8 %collective-permute-start.31 = (f32[16,768]{1,0:T(8,128)S(1)}, f32[16,768]{1,0:T(8,128)S(1)}, u32[]{:S(2)}, u32[]{:S(2)}) collective-permute-start(f32[16,768]{1,0:T(8,128)S(1)} %get-tuple-element.184.refs_7_), channel_id=1, source_target_pairs={{0,6},{1,7},{2,4},{3,5},{4,2},{5,3},{6,0},{7,1},{8,14},{9,15},{10,... | collective-permute-start | bytes 147464 | tf_op jit(solution)/shard_map/ppermute | solution.py:614
  160.5 4.7 %collective-permute-start.30 = (f32[16,768]{1,0:T(8,128)S(1)}, f32[16,768]{1,0:T(8,128)S(1)}, u32[]{:S(2)}, u32[]{:S(2)}) collective-permute-start(f32[16,768]{1,0:T(8,128)S(1)} %get-tuple-element.184.refs_7_), channel_id=1, source_target_pairs={{0,4},{1,5},{2,6},{3,7},{4,0},{5,1},{6,2},{7,3},{8,12},{9,13},{10,... | collective-permute-start | bytes 147464 | tf_op jit(solution)/shard_map/ppermute | solution.py:614
  162.1 5.7 %collective-permute-start.29 = (f32[16,768]{1,0:T(8,128)S(1)}, f32[16,768]{1,0:T(8,128)S(1)}, u32[]{:S(2)}, u32[]{:S(2)}) collective-permute-start(f32[16,768]{1,0:T(8,128)S(1)} %get-tuple-element.184.refs_7_), channel_id=1, source_target_pairs={{0,2},{1,3},{2,0},{3,1},{4,6},{5,7},{6,4},{7,5},{8,10},{9,11},{10,... | collective-permute-start | bytes 147464 | tf_op jit(solution)/shard_map/ppermute | solution.py:614
  163.3 29.5 %collective-permute-start.42 = (f32[8,3,48,128]{3,2,1,0:T(8,128)S(1)}, f32[8,3,48,128]{3,2,1,0:T(8,128)S(1)}, u32[]{:S(2)}, u32[]{:S(2)}) collective-permute-start(f32[8,3,48,128]{3,2,1,0:T(8,128)S(1)} %get-tuple-element.196), channel_id=1, source_target_pairs={{0,2},{1,5},{2,0},{3,7},{4,6},{5,1},{6,4},{7,3},{8,10},{9,13},{10,... | collective-permute-start | bytes 1769480 | tf_op jit(solution)/shard_map/ppermute | solution.py:614
  164.9 22.2 %collective-permute-start.33 = (f32[1,3,48,384]{3,2,1,0:T(8,128)S(1)}, f32[1,3,48,384]{3,2,1,0:T(8,128)S(1)}, u32[]{:S(2)}, u32[]{:S(2)}) collective-permute-start(f32[1,3,48,384]{3,2,1,0:T(8,128)S(1)} %get-tuple-element.176.refs_3_), channel_id=1, source_target_pairs={{0,16},{1,17},{2,18},{3,19},{4,20},{5,21},{6,22},{7,23},{8,24},{9,... | collective-permute-start | bytes 663560 | tf_op jit(solution)/shard_map/ppermute | solution.py:614
  165.3 13.1 %collective-permute-start.27 = (f32[1,1,48,384]{3,2,1,0:T(8,128)S(1)}, f32[1,1,48,384]{3,2,1,0:T(8,128)S(1)}, u32[]{:S(2)}, u32[]{:S(2)}) collective-permute-start(f32[1,1,48,384]{3,2,1,0:T(8,128)S(1)} %get-tuple-element.181), channel_id=1, source_target_pairs={{0,16},{1,17},{2,18},{3,19},{4,20},{5,21},{6,22},{7,23},{8,24},{9,... | collective-permute-start | bytes 221192 | tf_op jit(solution)/shard_map/ppermute | solution.py:614
  167.8 19.2 %collective-permute-start.34 = (f32[4,6,48,128]{3,2,1,0:T(8,128)S(1)}, f32[4,6,48,128]{3,2,1,0:T(8,128)S(1)}, u32[]{:S(2)}, u32[]{:S(2)}) collective-permute-start(f32[4,6,48,128]{3,2,1,0:T(8,128)S(1)} %get-tuple-element.177.refs_4_), channel_id=1, source_target_pairs={{0,2},{1,5},{2,0},{3,7},{4,6},{5,1},{6,4},{7,3},{8,10},{9,13},{10,... | collective-permute-start | bytes 1769480 | tf_op jit(solution)/shard_map/ppermute | solution.py:614
  179.0 13.1 %collective-permute-start.36 = (f32[1,3,48,384]{3,2,1,0:T(8,128)S(1)}, f32[1,3,48,384]{3,2,1,0:T(8,128)S(1)}, u32[]{:S(2)}, u32[]{:S(2)}) collective-permute-start(f32[1,3,48,384]{3,2,1,0:T(8,128)S(1)} %get-tuple-element.188.refs_5_), channel_id=1, source_target_pairs={{0,2},{1,5},{2,0},{3,7},{4,6},{5,1},{6,4},{7,3},{8,10},{9,13},{10,... | collective-permute-start | bytes 663560 | tf_op jit(solution)/shard_map/ppermute | solution.py:614
  180.0 5.9 %collective-permute-start.40 = (f32[16,768]{1,0:T(8,128)S(1)}, f32[16,768]{1,0:T(8,128)S(1)}, u32[]{:S(2)}, u32[]{:S(2)}) collective-permute-start(f32[16,768]{1,0:T(8,128)S(1)} %get-tuple-element.193.refs_5_), channel_id=1, source_target_pairs={{0,24},{1,25},{2,26},{3,27},{4,28},{5,29},{6,30},{7,31},{8,16},{9,... | collective-permute-start | bytes 147464 | tf_op jit(solution)/shard_map/ppermute | solution.py:614
  185.9 6.2 %collective-permute-start.37 = (f32[2,3,48,128]{3,2,1,0:T(8,128)S(1)}, f32[2,3,48,128]{3,2,1,0:T(8,128)S(1)}, u32[]{:S(2)}, u32[]{:S(2)}) collective-permute-start(f32[2,3,48,128]{3,2,1,0:T(8,128)S(1)} %get-tuple-element.192), channel_id=1, source_target_pairs={{0,2},{1,5},{2,0},{3,7},{4,6},{5,1},{6,4},{7,3},{8,10},{9,13},{10,... | collective-permute-start | bytes 442376 | tf_op jit(solution)/shard_map/ppermute | solution.py:614
  187.0 5.1 %collective-permute-start.39 = (f32[16,768]{1,0:T(8,128)S(1)}, f32[16,768]{1,0:T(8,128)S(1)}, u32[]{:S(2)}, u32[]{:S(2)}) collective-permute-start(f32[16,768]{1,0:T(8,128)S(1)} %get-tuple-element.193.refs_5_), channel_id=1, source_target_pairs={{0,16},{1,17},{2,18},{3,19},{4,20},{5,21},{6,22},{7,23},{8,24},{9,... | collective-permute-start | bytes 147464 | tf_op jit(solution)/shard_map/ppermute | solution.py:614
  187.0 5.1 %collective-permute-start.38 = (f32[16,768]{1,0:T(8,128)S(1)}, f32[16,768]{1,0:T(8,128)S(1)}, u32[]{:S(2)}, u32[]{:S(2)}) collective-permute-start(f32[16,768]{1,0:T(8,128)S(1)} %get-tuple-element.193.refs_5_), channel_id=1, source_target_pairs={{0,8},{1,9},{2,10},{3,11},{4,12},{5,13},{6,14},{7,15},{8,0},{9,1},... | collective-permute-start | bytes 147464 | tf_op jit(solution)/shard_map/ppermute | solution.py:614
  192.1 7.5 %collective-permute-start.45 = (f32[2,6,48,128]{3,2,1,0:T(8,128)S(1)}, f32[2,6,48,128]{3,2,1,0:T(8,128)S(1)}, u32[]{:S(2)}, u32[]{:S(2)}) collective-permute-start(f32[2,6,48,128]{3,2,1,0:T(8,128)S(1)} %get-tuple-element.202), channel_id=1, source_target_pairs={{0,8},{1,9},{2,10},{3,11},{4,12},{5,13},{6,14},{7,15},{8,0},{9,1},... | collective-permute-start | bytes 884744 | tf_op jit(solution)/shard_map/ppermute | solution.py:614
  193.4 6.8 %collective-permute-start.43 = (f32[4,3,48,128]{3,2,1,0:T(8,128)S(1)}, f32[4,3,48,128]{3,2,1,0:T(8,128)S(1)}, u32[]{:S(2)}, u32[]{:S(2)}) collective-permute-start(f32[4,3,48,128]{3,2,1,0:T(8,128)S(1)} %get-tuple-element.198.refs_7_), channel_id=1, source_target_pairs={{0,4},{1,3},{2,6},{3,1},{4,0},{5,7},{6,2},{7,5},{8,12},{9,11},{10,... | collective-permute-start | bytes 884744 | tf_op jit(solution)/shard_map/ppermute | solution.py:614
  194.3 5.4 %collective-permute-start.44 = (f32[1,3,48,128]{3,2,1,0:T(8,128)S(1)}, f32[1,3,48,128]{3,2,1,0:T(8,128)S(1)}, u32[]{:S(2)}, u32[]{:S(2)}) collective-permute-start(f32[1,3,48,128]{3,2,1,0:T(8,128)S(1)} %get-tuple-element.200), channel_id=1, source_target_pairs={{0,16},{1,17},{2,18},{3,19},{4,20},{5,21},{6,22},{7,23},{8,24},{9,... | collective-permute-start | bytes 221192 | tf_op jit(solution)/shard_map/ppermute | solution.py:614
  200.8 6.2 %collective-permute-start.48 = (f32[2,3,48,128]{3,2,1,0:T(8,128)S(1)}, f32[2,3,48,128]{3,2,1,0:T(8,128)S(1)}, u32[]{:S(2)}, u32[]{:S(2)}) collective-permute-start(f32[2,3,48,128]{3,2,1,0:T(8,128)S(1)} %get-tuple-element.207.refs_3_), channel_id=1, source_target_pairs={{0,8},{1,9},{2,10},{3,11},{4,12},{5,13},{6,14},{7,15},{8,0},{9,1},... | collective-permute-start | bytes 442376 | tf_op jit(solution)/shard_map/ppermute | solution.py:614
  203.0 7.6 %collective-permute-start.47 = (f32[1,6,48,128]{3,2,1,0:T(8,128)S(1)}, f32[1,6,48,128]{3,2,1,0:T(8,128)S(1)}, u32[]{:S(2)}, u32[]{:S(2)}) collective-permute-start(f32[1,6,48,128]{3,2,1,0:T(8,128)S(1)} %get-tuple-element.205), channel_id=1, source_target_pairs={{0,16},{1,17},{2,18},{3,19},{4,20},{5,21},{6,22},{7,23},{8,24},{9,... | collective-permute-start | bytes 442376 | tf_op jit(solution)/shard_map/ppermute | solution.py:614
  207.6 5.3 %collective-permute-start.49 = (f32[1,3,48,128]{3,2,1,0:T(8,128)S(1)}, f32[1,3,48,128]{3,2,1,0:T(8,128)S(1)}, u32[]{:S(2)}, u32[]{:S(2)}) collective-permute-start(f32[1,3,48,128]{3,2,1,0:T(8,128)S(1)} %get-tuple-element.209.refs_5_), channel_id=1, source_target_pairs={{0,16},{1,17},{2,18},{3,19},{4,20},{5,21},{6,22},{7,23},{8,24},{9,... | collective-permute-start | bytes 221192 | tf_op jit(solution)/shard_map/ppermute | solution.py:614
  209.6 3.9 %collective-permute-start.25 = (f32[1,1,48,384]{3,2,1,0:T(8,128)S(1)}, f32[1,1,48,384]{3,2,1,0:T(8,128)S(1)}, u32[]{:S(2)}, u32[]{:S(2)}) collective-permute-start(f32[1,1,48,384]{3,2,1,0:T(8,128)S(1)} %get-tuple-element.178.refs_1_), channel_id=1, source_target_pairs={{0,1},{1,0},{2,3},{3,2},{4,5},{5,4},{6,7},{7,6},{8,9},{9,8},{10,11... | collective-permute-start | bytes 221192 | tf_op jit(solution)/shard_map/ppermute | solution.py:614
  209.6 4.4 %collective-permute-start.32 = (f32[1,1,48,384]{3,2,1,0:T(8,128)S(1)}, f32[1,1,48,384]{3,2,1,0:T(8,128)S(1)}, u32[]{:S(2)}, u32[]{:S(2)}) collective-permute-start(f32[1,1,48,384]{3,2,1,0:T(8,128)S(1)} %get-tuple-element.185.refs_3_), channel_id=1, source_target_pairs={{0,1},{1,0},{2,3},{3,2},{4,5},{5,4},{6,7},{7,6},{8,9},{9,8},{10,11... | collective-permute-start | bytes 221192 | tf_op jit(solution)/shard_map/ppermute | solution.py:614
  210.2 4.0 %collective-permute-start.41 = (f32[1,3,48,384]{3,2,1,0:T(8,128)S(1)}, f32[1,3,48,384]{3,2,1,0:T(8,128)S(1)}, u32[]{:S(2)}, u32[]{:S(2)}) collective-permute-start(f32[1,3,48,384]{3,2,1,0:T(8,128)S(1)} %get-tuple-element.194.refs_3_.refs_7_), channel_id=1, source_target_pairs={{0,1},{1,0},{2,3},{3,2},{4,5},{5,4},{6,7},{7,6},{8,9},{9,8},{10,11... | collective-permute-start | bytes 663560 | tf_op jit(solution)/shard_map/ppermute | solution.py:614
  210.6 3.6 %collective-permute-start.35 = (f32[1,3,48,384]{3,2,1,0:T(8,128)S(1)}, f32[1,3,48,384]{3,2,1,0:T(8,128)S(1)}, u32[]{:S(2)}, u32[]{:S(2)}) collective-permute-start(f32[1,3,48,384]{3,2,1,0:T(8,128)S(1)} %get-tuple-element.189.refs_9_.refs_5_), channel_id=1, source_target_pairs={{0,1},{1,0},{2,3},{3,2},{4,5},{5,4},{6,7},{7,6},{8,9},{9,8},{10,11... | collective-permute-start | bytes 663560 | tf_op jit(solution)/shard_map/ppermute | solution.py:614
  (21 other events, 189.8 us)
